TPU v7x, 32 devices: a whole 2x2x4 slice. The times are simulated.
32 devices in a mesh: ctx: 8 (over y, x, core), fsdp: 4 (over z).
Axes of the slice: x: 2, y: 2, z: 4, core: 2. Of those that a mesh axis runs over, the one named last changes fastest.
Arguments:
- hidden_in: bfloat16 [4, 2048, 1024], P('fsdp', 'ctx'), may hold values from -6 to 6
- seq_lengths: int32 [4, 4], P('fsdp'), may hold values from 1 to 1024, 1984 in all within a row
- in_gain: bfloat16 [1024], P(('ctx', 'fsdp')), may hold values from 0.5 to 1.5
- w_query: bfloat16 [1024, 2048], P(('ctx', 'fsdp')), may hold values from -0.1875 to 0.1875
- w_key: bfloat16 [1024, 1024], P(('ctx', 'fsdp')), may hold values from -0.1875 to 0.1875
- w_value: bfloat16 [1024, 1024], P(('ctx', 'fsdp')), may hold values from -0.1875 to 0.1875
- q_gain: bfloat16 [128], P(('ctx', 'fsdp')), may hold values from 0.5 to 1.5
- k_gain: bfloat16 [128], P(('ctx', 'fsdp')), may hold values from 0.5 to 1.5
- w_out: bfloat16 [2048, 1024], P(('ctx', 'fsdp')), may hold values from -1.5 to 1.5
- post_gain: bfloat16 [1024], P(('ctx', 'fsdp')), may hold values from 0.5 to 1.5
- w_gate: bfloat16 [1024, 3072], P(('ctx', 'fsdp')), may hold values from -0.1875 to 0.1875
- w_up: bfloat16 [1024, 3072], P(('ctx', 'fsdp')), may hold values from -0.1875 to 0.1875
- w_down: bfloat16 [3072, 1024], P(('ctx', 'fsdp')), may hold values from -0.109375 to 0.109375
- d_out: bfloat16 [4, 2048, 1024], P('fsdp', 'ctx'), may hold values from -6 to 6
Outputs:
- block_out: bfloat16 [4, 2048, 1024], P('fsdp', 'ctx')
- d_hidden: float32 [4, 2048, 1024], P('fsdp', 'ctx')
- grad_in_gain: float32 [1024], P(('ctx', 'fsdp'))
- grad_w_query: float32 [1024, 2048], P(('ctx', 'fsdp'))
- grad_w_key: float32 [1024, 1024], P(('ctx', 'fsdp'))
- grad_w_value: float32 [1024, 1024], P(('ctx', 'fsdp'))
- grad_q_gain: float32 [128], P(('ctx', 'fsdp'))
- grad_k_gain: float32 [128], P(('ctx', 'fsdp'))
- grad_w_out: float32 [2048, 1024], P(('ctx', 'fsdp'))
- grad_post_gain: float32 [1024], P(('ctx', 'fsdp'))
- grad_w_gate: float32 [1024, 3072], P(('ctx', 'fsdp'))
- grad_w_up: float32 [1024, 3072], P(('ctx', 'fsdp'))
- grad_w_down: float32 [3072, 1024], P(('ctx', 'fsdp'))
Inputs may be any that keep to these rules, and one draw needn't show every extreme that they name: `seq_lengths`: in every group the 4 lengths sum to 1984, and the longest is exactly 1024.
All inputs are finite; a program needn't handle non-finite values.
Results may differ from a plain program's by a relative error of at most 0.019.
Values may be sent and summed in bfloat16 or wider, within the bound.
A program may use at most 320 MiB of HBM per device.

v0:
```python
import jax
import jax.numpy as jnp
from jax import lax
from jax.sharding import PartitionSpec as P

epsilon = 1e-06
rope_base = 1000000.0
negative = -1e30


def row_info(lengths, row_ids, tok_dev, n_ctx):
    half_len = tok_dev // 2
    device = row_ids // tok_dev
    local_row = row_ids % tok_dev
    block_id = jnp.where(local_row < half_len, device, 2 * n_ctx - 1 - device)
    packed = block_id * half_len + local_row % half_len
    seq_ends = jnp.cumsum(lengths)
    seq_starts = seq_ends - lengths
    member = (packed[:, None] >= seq_starts[None, :]) & (packed[:, None] < seq_ends[None, :])
    row_valid = jnp.any(member, axis=1)
    numbers = jnp.arange(lengths.shape[0], dtype=jnp.int32)
    seq_id = jnp.sum(jnp.where(member, numbers[None, :], 0), axis=1)
    offset = jnp.sum(jnp.where(member, seq_starts[None, :], 0), axis=1)
    segment = jnp.where(row_valid, seq_id, -1 - packed)
    position = jnp.where(row_valid, packed - offset, 0)
    return (segment, position, row_valid)


def norm_gain(values_in, gain_vec):
    row_scale = lax.rsqrt(jnp.mean(values_in * values_in, axis=-1, keepdims=True) + epsilon)
    return values_in * row_scale * gain_vec


def rotary(position, head_dim):
    half_len = head_dim // 2
    inv_freq = jnp.power(rope_base, -jnp.arange(half_len, dtype=jnp.float32) * (2.0 / head_dim))
    angles = position.astype(jnp.float32)[:, None] * inv_freq[None, :]
    angles = jnp.concatenate([angles, angles], axis=1)
    return (jnp.cos(angles), jnp.sin(angles))


def rotate(heads, cos_table, sin_table):
    half_len = heads.shape[-1] // 2
    turned = jnp.concatenate([-heads[..., half_len:], heads[..., :half_len]], axis=-1)
    return heads * cos_table[:, None, :] + turned * sin_table[:, None, :]


def head_post(q_in, k_in, q_scale, k_scale, cos_table, sin_table):
    head_dim = q_scale.shape[0]
    row_count = q_in.shape[0]
    q_heads = norm_gain(q_in.reshape(row_count, -1, head_dim), q_scale)
    k_heads = norm_gain(k_in.reshape(row_count, -1, head_dim), k_scale)
    query_rotated = rotate(q_heads, cos_table, sin_table).reshape(row_count, -1)
    key_rotated = rotate(k_heads, cos_table, sin_table).reshape(row_count, -1)
    return (query_rotated, key_rotated)


def swiglu(gate_in, up_in):
    return jax.nn.silu(gate_in) * up_in


def matmul(left, right):
    return jnp.dot(left, right, preferred_element_type=jnp.float32)


def inner(left, right):
    return lax.dot_general(
        left, right, (((0,), (0,)), ((), ())), preferred_element_type=jnp.float32
    )


def backdot(left, right):
    return lax.dot_general(
        left, right, (((1,), (1,)), ((), ())), preferred_element_type=jnp.float32
    )


def pick_step(key_count):
    for candidate in (512, 384, 256):
        return candidate
    return key_count


def on_device(
    hidden_in,
    seq_lengths,
    in_gain,
    w_query,
    w_key,
    w_value,
    q_gain,
    k_gain,
    w_out,
    post_gain,
    w_gate,
    w_up,
    w_down,
    d_out,
):
    n_ctx = lax.axis_size("ctx")
    row_count = hidden_in.shape[1]
    lengths = seq_lengths[0]
    own_rows = lax.axis_index("ctx") * row_count + jnp.arange(row_count, dtype=jnp.int32)
    seg_q, pos_q, row_valid = row_info(lengths, own_rows, row_count, n_ctx)
    shards = (
        in_gain,
        w_query,
        w_key,
        w_value,
        q_gain,
        k_gain,
        w_out,
        post_gain,
        w_gate,
        w_up,
        w_down,
    )
    gathered = (
        lax.all_gather(shards[0], ("ctx", "fsdp"), axis=0, tiled=True),
        lax.all_gather(shards[1], ("ctx", "fsdp"), axis=0, tiled=True),
        lax.all_gather(shards[2], ("ctx", "fsdp"), axis=0, tiled=True),
        lax.all_gather(shards[3], ("ctx", "fsdp"), axis=0, tiled=True),
        lax.all_gather(shards[4], ("ctx", "fsdp"), axis=0, tiled=True),
        lax.all_gather(shards[5], ("ctx", "fsdp"), axis=0, tiled=True),
        lax.all_gather(shards[6], ("ctx", "fsdp"), axis=0, tiled=True),
        lax.all_gather(shards[7], ("ctx", "fsdp"), axis=0, tiled=True),
        lax.all_gather(shards[8], ("ctx", "fsdp"), axis=0, tiled=True),
        lax.all_gather(shards[9], ("ctx", "fsdp"), axis=0, tiled=True),
        lax.all_gather(shards[10], ("ctx", "fsdp"), axis=0, tiled=True),
    )
    g_in = gathered[0].astype(jnp.float32)
    g_query = gathered[4].astype(jnp.float32)
    g_key = gathered[5].astype(jnp.float32)
    g_post = gathered[7].astype(jnp.float32)
    head_dim = gathered[4].shape[0]
    kv_width = gathered[2].shape[1]
    kv_heads = kv_width // head_dim
    group_count = gathered[1].shape[1] // kv_width
    score_scale = head_dim ** (-0.5)
    rows_per_group = row_count * n_ctx
    x_float = hidden_in[0].astype(jnp.float32)
    x_normf, in_back = jax.vjp(norm_gain, x_float, g_in)
    x_norm = x_normf.astype(jnp.bfloat16)
    q_pre = matmul(x_norm, gathered[1])
    k_pre = matmul(x_norm, gathered[2])
    value_projected = matmul(x_norm, gathered[3])
    cos_table, sin_table = rotary(pos_q, head_dim)

    def post_local(q_in, k_in, q_scale, k_scale):
        return head_post(q_in, k_in, q_scale, k_scale, cos_table, sin_table)

    rotated, post_back = jax.vjp(post_local, q_pre, k_pre, g_query, g_key)
    q_low4 = rotated[0].astype(jnp.bfloat16).reshape(row_count, kv_heads, group_count, head_dim)
    key_narrow = rotated[1].astype(jnp.bfloat16)
    value_narrow = value_projected.astype(jnp.bfloat16)

    def sweep_keys(carry, k_piece, v_piece, block_fn):
        key_count = k_piece.shape[0]
        key_step = pick_step(key_count)

        def one_turn(state, turn_index):
            offset = turn_index * key_step
            k_block = lax.dynamic_slice_in_dim(k_piece, offset, key_step, 0)
            v_block = lax.dynamic_slice_in_dim(v_piece, offset, key_step, 0)
            key_rows = offset + jnp.arange(key_step, dtype=jnp.int32)
            seg_k, pos_k, unused = row_info(lengths, key_rows, row_count, n_ctx)
            allowed = (seg_q[:, None] == seg_k[None, :]) & (pos_k[None, :] <= pos_q[:, None])
            state = block_fn(state, k_block, v_block, allowed, offset)
            return (state, None)

        carry, unused = lax.scan(
            one_turn, carry, jnp.arange(key_count // key_step, dtype=jnp.int32)
        )
        return carry

    def forward_block(carry, k_block, v_block, allowed, first_key):
        row_max, totals, weighted = carry
        k_heads = k_block.reshape(-1, kv_heads, head_dim)
        v_heads = v_block.reshape(-1, kv_heads, head_dim)
        mask_four = allowed[None, None]
        score = (
            jnp.einsum("qhgd,khd->hgqk", q_low4, k_heads, preferred_element_type=jnp.float32)
            * score_scale
        )
        block_max = jnp.max(jnp.where(mask_four, score, negative), axis=-1)
        new_max = jnp.maximum(row_max, block_max)
        expo = jnp.where(mask_four, jnp.exp(score - new_max[..., None]), 0.0)
        factor = jnp.exp(row_max - new_max)
        totals = totals * factor + jnp.sum(expo, axis=-1)
        weighted = weighted * factor[..., None] + jnp.einsum(
            "hgqk,khd->hgqd", expo.astype(jnp.bfloat16), v_heads, preferred_element_type=jnp.float32
        )
        return (new_max, totals, weighted)

    start_state = (
        jnp.full((kv_heads, group_count, row_count), negative, jnp.float32),
        jnp.zeros((kv_heads, group_count, row_count), jnp.float32),
        jnp.zeros((kv_heads, group_count, row_count, head_dim), jnp.float32),
    )
    pieces = (
        lax.all_gather(key_narrow, "ctx", axis=0, tiled=True),
        lax.all_gather(value_narrow, "ctx", axis=0, tiled=True),
    )
    fold_state = sweep_keys(start_state, pieces[0], pieces[1], forward_block)
    row_max, totals, weighted = fold_state
    attn_four = weighted / totals[..., None]
    log_total = row_max + jnp.log(totals)
    attn = jnp.transpose(attn_four, (2, 0, 1, 3)).reshape(row_count, -1)
    attn_low = attn.astype(jnp.bfloat16)
    h_mid = x_float + matmul(attn_low, gathered[6])
    h_normf, post_norm_back = jax.vjp(norm_gain, h_mid, g_post)
    h_norm = h_normf.astype(jnp.bfloat16)
    gate_out = matmul(h_norm, gathered[8])
    up_out = matmul(h_norm, gathered[9])
    act_float, swiglu_back = jax.vjp(swiglu, gate_out, up_out)
    act_low = act_float.astype(jnp.bfloat16)
    row_mask = row_valid.astype(jnp.float32)[:, None]
    block_out = (row_mask * (h_mid + matmul(act_low, gathered[10]))).astype(jnp.bfloat16)
    again = (
        lax.all_gather(shards[0], ("ctx", "fsdp"), axis=0, tiled=True),
        lax.all_gather(shards[1], ("ctx", "fsdp"), axis=0, tiled=True),
        lax.all_gather(shards[2], ("ctx", "fsdp"), axis=0, tiled=True),
        lax.all_gather(shards[3], ("ctx", "fsdp"), axis=0, tiled=True),
        lax.all_gather(shards[4], ("ctx", "fsdp"), axis=0, tiled=True),
        lax.all_gather(shards[5], ("ctx", "fsdp"), axis=0, tiled=True),
        lax.all_gather(shards[6], ("ctx", "fsdp"), axis=0, tiled=True),
        lax.all_gather(shards[7], ("ctx", "fsdp"), axis=0, tiled=True),
        lax.all_gather(shards[8], ("ctx", "fsdp"), axis=0, tiled=True),
        lax.all_gather(shards[9], ("ctx", "fsdp"), axis=0, tiled=True),
        lax.all_gather(shards[10], ("ctx", "fsdp"), axis=0, tiled=True),
    )
    d_block = d_out[0].astype(jnp.float32) * row_mask
    dm_low = d_block.astype(jnp.bfloat16)
    grad_down = inner(act_low, dm_low)
    d_act = backdot(dm_low, again[10])
    d_gate, d_up = swiglu_back(d_act)
    dg_low = d_gate.astype(jnp.bfloat16)
    du_low = d_up.astype(jnp.bfloat16)
    grad_gate = inner(h_norm, dg_low)
    grad_up = inner(h_norm, du_low)
    d_hnorm = backdot(dg_low, again[8]) + backdot(du_low, again[9])
    d_hpart, grad_post = post_norm_back(d_hnorm)
    d_hmid = d_block + d_hpart
    d_res = d_hmid.astype(jnp.bfloat16)
    grad_wout = inner(attn_low, d_res)
    d_attn = backdot(d_res, again[6]).astype(jnp.bfloat16)
    d_attn4 = d_attn.reshape(row_count, kv_heads, group_count, head_dim)
    delta = jnp.einsum("qhgd,hgqd->hgq", d_attn4.astype(jnp.float32), attn_four)

    def backward_block(carry, k_block, v_block, allowed, first_key):
        d_query, d_kv = carry
        key_count = k_block.shape[0]
        k_heads = k_block.reshape(-1, kv_heads, head_dim)
        v_heads = v_block.reshape(-1, kv_heads, head_dim)
        mask_four = allowed[None, None]
        score = (
            jnp.einsum("qhgd,khd->hgqk", q_low4, k_heads, preferred_element_type=jnp.float32)
            * score_scale
        )
        prob = jnp.where(mask_four, jnp.exp(score - log_total[..., None]), 0.0)
        prob_low = prob.astype(jnp.bfloat16)
        d_prob = jnp.einsum("qhgd,khd->hgqk", d_attn4, v_heads, preferred_element_type=jnp.float32)
        d_score = (prob * (d_prob - delta[..., None])).astype(jnp.bfloat16)
        d_query = d_query + jnp.einsum(
            "hgqk,khd->qhgd", d_score, k_heads, preferred_element_type=jnp.float32
        )
        d_key = (
            jnp.einsum("hgqk,qhgd->khd", d_score, q_low4, preferred_element_type=jnp.float32)
            * score_scale
        )
        d_value = jnp.einsum(
            "hgqk,qhgd->khd", prob_low, d_attn4, preferred_element_type=jnp.float32
        )
        joined = jnp.concatenate(
            [d_key.reshape(key_count, -1), d_value.reshape(key_count, -1)], axis=1
        )
        before = lax.dynamic_slice_in_dim(d_kv, first_key, key_count, 0)
        d_kv = lax.dynamic_update_slice_in_dim(d_kv, before + joined, first_key, 0)
        return (d_query, d_kv)

    back_start = (
        jnp.zeros((row_count, kv_heads, group_count, head_dim), jnp.float32),
        jnp.zeros((rows_per_group, 2 * kv_width), jnp.float32),
    )
    pieces = (
        lax.all_gather(key_narrow, "ctx", axis=0, tiled=True),
        lax.all_gather(value_narrow, "ctx", axis=0, tiled=True),
    )
    back_state = sweep_keys(back_start, pieces[0], pieces[1], backward_block)
    d_qrot = back_state[0].reshape(row_count, -1) * score_scale
    d_kv_own = lax.psum_scatter(
        back_state[1].astype(jnp.bfloat16), "ctx", scatter_dimension=0, tiled=True
    ).astype(jnp.float32)
    d_krot = d_kv_own[:, :kv_width]
    d_vpre = d_kv_own[:, kv_width:]
    d_qpre, d_kpre, grad_qgain, grad_kgain = post_back((d_qrot, d_krot))
    dq_low = d_qpre.astype(jnp.bfloat16)
    dk_low = d_kpre.astype(jnp.bfloat16)
    dv_low = d_vpre.astype(jnp.bfloat16)
    grad_query = inner(x_norm, dq_low)
    grad_key = inner(x_norm, dk_low)
    grad_value = inner(x_norm, dv_low)
    d_xnorm = backdot(dq_low, again[1]) + backdot(dk_low, again[2]) + backdot(dv_low, again[3])
    d_xpart, grad_ingain = in_back(d_xnorm)
    d_hidden = d_hmid + d_xpart
    owned = (
        lax.psum_scatter(grad_ingain, ("ctx", "fsdp"), scatter_dimension=0, tiled=True),
        lax.psum_scatter(grad_query, ("ctx", "fsdp"), scatter_dimension=0, tiled=True),
        lax.psum_scatter(grad_key, ("ctx", "fsdp"), scatter_dimension=0, tiled=True),
        lax.psum_scatter(grad_value, ("ctx", "fsdp"), scatter_dimension=0, tiled=True),
        lax.psum_scatter(grad_qgain, ("ctx", "fsdp"), scatter_dimension=0, tiled=True),
        lax.psum_scatter(grad_kgain, ("ctx", "fsdp"), scatter_dimension=0, tiled=True),
        lax.psum_scatter(grad_wout, ("ctx", "fsdp"), scatter_dimension=0, tiled=True),
        lax.psum_scatter(grad_post, ("ctx", "fsdp"), scatter_dimension=0, tiled=True),
        lax.psum_scatter(grad_gate, ("ctx", "fsdp"), scatter_dimension=0, tiled=True),
        lax.psum_scatter(grad_up, ("ctx", "fsdp"), scatter_dimension=0, tiled=True),
        lax.psum_scatter(grad_down, ("ctx", "fsdp"), scatter_dimension=0, tiled=True),
    )
    return (
        block_out[None],
        d_hidden[None],
        owned[0],
        owned[1],
        owned[2],
        owned[3],
        owned[4],
        owned[5],
        owned[6],
        owned[7],
        owned[8],
        owned[9],
        owned[10],
    )


def solution(mesh):
    in_specs = (
        P("fsdp", "ctx", None),
        P("fsdp", None),
        P(("ctx", "fsdp")),
        P(("ctx", "fsdp"), None),
        P(("ctx", "fsdp"), None),
        P(("ctx", "fsdp"), None),
        P(("ctx", "fsdp")),
        P(("ctx", "fsdp")),
        P(("ctx", "fsdp"), None),
        P(("ctx", "fsdp")),
        P(("ctx", "fsdp"), None),
        P(("ctx", "fsdp"), None),
        P(("ctx", "fsdp"), None),
        P("fsdp", "ctx", None),
    )
    out_specs = (
        P("fsdp", "ctx", None),
        P("fsdp", "ctx", None),
        P(("ctx", "fsdp")),
        P(("ctx", "fsdp"), None),
        P(("ctx", "fsdp"), None),
        P(("ctx", "fsdp"), None),
        P(("ctx", "fsdp")),
        P(("ctx", "fsdp")),
        P(("ctx", "fsdp"), None),
        P(("ctx", "fsdp")),
        P(("ctx", "fsdp"), None),
        P(("ctx", "fsdp"), None),
        P(("ctx", "fsdp"), None),
    )
    return jax.shard_map(
        on_device, mesh=mesh, in_specs=in_specs, out_specs=out_specs, check_vma=False
    )
```

profile of v0, /device:TPU:0, one launch (start us, length us, event | category | flops | bytes accessed | tf_op | source)
XLA Modules:
  0.0 1904.4 jit_solution(9083443953777462207)
XLA Ops:
  12.8 42.2 %all-reduce.13 = (bf16[1024]{0:T(1024)(128)(2,1)S(1)}, bf16[128]{0:T(256)(128)(2,1)S(1)}, bf16[128]{0:T(256)(128)(2,1)S(1)}, bf16[1024]{0:T(1024)(128)(2,1)S(1)}) all-reduce(bf16[1024]{0:T(1024)(128)(2,1)S(1)} %dynamic-update-slice, bf16[128]{0:T(256)(128)(2,1)S(1)} %dynamic-update-slice.1, ...), channel_id=1, replica_groups=mesh['ctx'=8,'fsdp'=4] {'ctx','fsdp'}, use_global_device_ids=true, to_apply=%add.4 | all-reduce | flops 2304 | bytes 9216
  56.3 13.9 all-gather.16.cloned.1.call-done
  70.2 3.3 convolution_convert_fusion.1
  75.3 53.2 %all-gather.10.cloned.1.call-done = bf16[1024,1024]{1,0:T(8,128)(2,1)} async-done(((bf16[32,1024]{1,0:T(8,128)(2,1)}), bf16[1024,1024]{1,0:T(8,128)(2,1)}) %all-gather.10.cloned.1.call-update) | async-done | bytes 2097168 | tf_op jit(solution)/shard_map/all_gather | solution.py:121
  128.5 2.9 copy.83
  137.1 55.3 %all-gather.14.cloned.1.call-done = bf16[1024,2048]{1,0:T(8,128)(2,1)} async-done(((bf16[32,2048]{1,0:T(8,128)(2,1)}), bf16[1024,2048]{1,0:T(8,128)(2,1)}) %all-gather.14.cloned.1.call-update) | async-done | bytes 4194320 | tf_op jit(solution)/shard_map/all_gather | solution.py:120
  192.5 6.5 copy.84
  199.0 3.9 multiply_reduce_fusion.3
  206.1 23.4 %all-gather.18.cloned.1.call-done = bf16[2048,1024]{1,0:T(8,128)(2,1)} async-done(((bf16[256,1024]{1,0:T(8,128)(2,1)}), bf16[2048,1024]{1,0:T(8,128)(2,1)}) %all-gather.18.cloned.1.call-update) | async-done | bytes 4194320 | tf_op jit(solution)/shard_map/all_gather | solution.py:202
  229.5 6.6 copy.86
  236.1 33.2 %all-gather.12.cloned.1.call-done = bf16[2048,1024]{0,1:T(8,128)(2,1)} async-done(((bf16[256,1024]{0,1:T(8,128)(2,1)}), bf16[2048,1024]{0,1:T(8,128)(2,1)}) %all-gather.12.cloned.1.call-update) | async-done | bytes 4194320 | tf_op jit(solution)/shard_map/all_gather | solution.py:201
  269.3 45.1 %while.34 = (s32[]{:T(128)}, f32[8,2,256]{2,1,0:T(2,128)S(1)}, f32[8,2,256]{2,1,0:T(2,128)S(1)}, f32[8,2,256,128]{3,2,1,0:T(8,128)}, s32[256]{0:T(256)S(1)}, /*i...) while((s32[]{:T(128)}, f32[8,2,256]{2,1,0:T(2,128)S(1)}, ...), condition=%wide.region_13.14_spmd.clone, body=%wide.region_7.13_spmd.clone.sunk | while | flops 1098850816 | bytes 58486120 | solution.py:171
  276.1 3.2 fusion.197
  287.3 3.2 fusion.197
  298.6 3.2 fusion.197
  309.9 3.2 fusion.197
  314.4 3.4 copy.87
  317.8 2.8 fusion.76
  320.6 13.7 all-gather.20.cloned.1.call-done
  334.3 4.0 multiply_reduce_fusion.8
  340.1 65.1 %all-gather.24.cloned.1.call-done = bf16[1024,3072]{1,0:T(8,128)(2,1)} async-done(((bf16[32,3072]{1,0:T(8,128)(2,1)}), bf16[1024,3072]{1,0:T(8,128)(2,1)}) %all-gather.24.cloned.1.call-update) | async-done | bytes 6291472 | tf_op jit(solution)/shard_map/all_gather | solution.py:128
  405.3 6.5 fusion.116
  411.7 64.5 %all-gather.22.cloned.1.call-done = bf16[1024,3072]{1,0:T(8,128)(2,1)} async-done(((bf16[32,3072]{1,0:T(8,128)(2,1)}), bf16[1024,3072]{1,0:T(8,128)(2,1)}) %all-gather.22.cloned.1.call-update) | async-done | bytes 6291472 | tf_op jit(solution)/shard_map/all_gather | solution.py:127
  476.3 6.4 fusion.115
  482.7 64.5 %all-gather.26.cloned.1.call-done = bf16[3072,1024]{1,0:T(8,128)(2,1)} async-done(((bf16[96,1024]{1,0:T(8,128)(2,1)}), bf16[3072,1024]{1,0:T(8,128)(2,1)}) %all-gather.26.cloned.1.call-update) | async-done | bytes 6291472 | tf_op jit(solution)/shard_map/all_gather | solution.py:129
  547.2 9.1 multiply_convert_fusion
  558.4 5.8 multiply_reduce_fusion.4
  565.6 2.6 convolution_convert_fusion
  568.1 2.6 reshape.692
  570.7 3.6 copy.89
  574.3 3.3 bitcast_convert_fusion
  577.7 4.1 copy.107
  581.8 2.6 multiply_reduce_fusion
  584.4 7.9 broadcast_in_dim.194
  592.3 68.2 %while.35 = (s32[]{:T(128)}, f32[256,8,2,128]{0,3,2,1:T(8,128)S(1)}, f32[2048,2048]{0,1:T(8,128)}, s32[4]{0:T(128)S(1)}, bf16[2048,1024]{0,1:T(8,128)(2,1)}, /*i...) while((s32[]{:T(128)}, ...), condition=%wide.region_20.21_spmd.clone, body=%wide.region_16.20_spmd.clone.sunk | while | flops 2709443072 | bytes 74919232 | solution.py:171
  596.9 1.8 fusion.211
  598.7 2.9 fusion.210
  604.1 5.2 fusion.212
  615.8 2.9 fusion.210
  621.2 5.2 fusion.212
  632.8 2.9 fusion.210
  638.1 5.2 fusion.212
  648.0 1.8 fusion.211
  649.8 2.9 fusion.210
  655.2 5.3 fusion.212
  660.4 9.1 convert_element_type.177
  670.7 6.3 fusion.88
  677.1 9.2 fusion.91
  686.3 8.3 fusion.120
  694.7 8.1 fusion.119
  708.2 4.8 fusion.83
  713.0 26.4 %reduce-scatter.9.cloned.1.call-done = bf16[256,2048]{0,1:T(8,128)(2,1)} async-done(((bf16[2048,2048]{0,1:T(8,128)(2,1)}), bf16[256,2048]{0,1:T(8,128)(2,1)}) %reduce-scatter.9.cloned.1.call-update) | async-done | bytes 1048592 | tf_op jit(solution)/shard_map/reduce_scatter | solution.py:291
  739.5 3.9 fusion.85
  746.5 2.8 fusion.81
  750.5 3.6 fusion.118
  754.2 5.6 fusion.60
  762.7 42.2 %all-reduce.12 = (f32[1024]{0:T(1024)S(1)}, f32[128]{0:T(128)S(1)}, f32[128]{0:T(128)S(1)}, f32[1024]{0:T(1024)S(1)}) all-reduce(f32[1024]{0:T(1024)S(1)} %get-tuple-element.623, f32[128]{0:T(128)S(1)} %get-tuple-element.617, f32[128]{0:T(128)S(1)} %get-tuple-element.619, ...), channel_id=3, replica_groups=mesh['ctx'=8,'fsdp'=4] {'ctx','fsdp'}, use_global_device_ids=true, to_apply=%region_26.27.clone | all-reduce | flops 2304 | bytes 18432
  808.6 120.7 %reduce-scatter.17.cloned.1.call-done = f32[64,1024]{1,0:T(8,128)} async-done(((f32[2048,1024]{1,0:T(8,128)}), f32[64,1024]{1,0:T(8,128)}) %reduce-scatter.17.cloned.1.call-update) | async-done | bytes 262160 | tf_op jit(solution)/shard_map/reduce_scatter | solution.py:313
  929.3 160.6 %reduce-scatter.23.cloned.1.call-done = f32[96,1024]{1,0:T(8,128)} async-done(((f32[3072,1024]{1,0:T(8,128)}), f32[96,1024]{1,0:T(8,128)}) %reduce-scatter.23.cloned.1.call-update) | async-done | bytes 393232 | tf_op jit(solution)/shard_map/reduce_scatter | solution.py:317
  1089.9 161.1 %reduce-scatter.21.cloned.1.call-done = f32[32,3072]{1,0:T(8,128)} async-done(((f32[1024,3072]{1,0:T(8,128)}), f32[32,3072]{1,0:T(8,128)}) %reduce-scatter.21.cloned.1.call-update) | async-done | bytes 393232 | tf_op jit(solution)/shard_map/reduce_scatter | solution.py:316
  1251.0 162.0 %reduce-scatter.19.cloned.1.call-done = f32[32,3072]{1,0:T(8,128)} async-done(((f32[1024,3072]{1,0:T(8,128)}), f32[32,3072]{1,0:T(8,128)}) %reduce-scatter.19.cloned.1.call-update) | async-done | bytes 393232 | tf_op jit(solution)/shard_map/reduce_scatter | solution.py:315
  1413.0 187.7 %reduce-scatter.11.cloned.1.call-done = f32[32,2048]{1,0:T(8,128)} async-done(((f32[1024,2048]{1,0:T(8,128)}), f32[32,2048]{1,0:T(8,128)}) %reduce-scatter.11.cloned.1.call-update) | async-done | bytes 262160 | tf_op jit(solution)/shard_map/reduce_scatter | solution.py:308
  1600.7 148.1 %reduce-scatter.15.cloned.1.call-done = f32[32,1024]{1,0:T(8,128)} async-done(((f32[1024,1024]{1,0:T(8,128)}), f32[32,1024]{1,0:T(8,128)}) %reduce-scatter.15.cloned.1.call-update) | async-done | bytes 131088 | tf_op jit(solution)/shard_map/reduce_scatter | solution.py:310
  1748.7 148.9 %reduce-scatter.13.cloned.1.call-done = f32[32,1024]{1,0:T(8,128)} async-done(((f32[1024,1024]{1,0:T(8,128)}), f32[32,1024]{1,0:T(8,128)}) %reduce-scatter.13.cloned.1.call-update) | async-done | bytes 131088 | tf_op jit(solution)/shard_map/reduce_scatter | solution.py:309
  (320 shorter events, 98.5 us)
Async XLA Ops:
  7.2 66.5 %copy-start.52 = (s32[1,4]{1,0:T(1,128)S(1)}, s32[1,4]{1,0:T(1,128)}, u32[]{:S(2)}) copy-start(s32[1,4]{1,0:T(1,128)} %param.19) | copy-start | bytes 52
  7.2 63.0 %all-gather.16.cloned.1.call-start = ((), (), s32[]{:S(2)}) async-start(), calls=%async_computation.11 | async-start | bytes 2162688 | tf_op jit(solution)/shard_map/all_gather | solution.py:122
  7.9 120.6 %all-gather.10.cloned.1.call-start = ((), (), s32[]{:S(2)}) async-start(), calls=%async_computation.8 | async-start | bytes 2162688 | tf_op jit(solution)/shard_map/all_gather | solution.py:121
  8.7 183.8 %all-gather.14.cloned.1.call-start = ((), (), s32[]{:S(2)}) async-start(), calls=%async_computation.10 | async-start | bytes 4325376 | tf_op jit(solution)/shard_map/all_gather | solution.py:120
  9.4 220.1 %all-gather.18.cloned.1.call-start = ((), (), s32[]{:S(2)}) async-start(), calls=%async_computation.12 | async-start | bytes 4718592 | tf_op jit(solution)/shard_map/all_gather | solution.py:202
  55.1 143.9 %copy-start.32 = (f32[1024]{0:T(1024)}, f32[1024]{0:T(1024)S(1)}, u32[]{:S(2)}) copy-start(f32[1024]{0:T(1024)S(1)} %convert_element_type.149) | copy-start | bytes 12292
  56.3 17.7 copy-start.42
  56.3 142.6 %copy-start.38 = (f32[256]{0:T(256)}, f32[256]{0:T(256)S(1)}, u32[]{:S(2)}) copy-start(f32[256]{0:T(256)S(1)} %fusion.104) | copy-start | bytes 3076
  73.5 57.8 %copy-start.5 = (bf16[1,256,1024]{2,1,0:T(8,128)(2,1)S(1)}, bf16[1,256,1024]{2,1,0:T(8,128)(2,1)}, u32[]{:S(2)}) copy-start(bf16[1,256,1024]{2,1,0:T(8,128)(2,1)} %param.18) | copy-start | bytes 1572868
  73.6 195.7 %all-gather.12.cloned.1.call-start = ((), (), s32[]{:S(2)}) async-start(), calls=%async_computation.9 | async-start | bytes 4718592 | tf_op jit(solution)/shard_map/all_gather | solution.py:201
  73.6 58.9 %copy-start.44 = (f32[128]{0:T(128)}, f32[128]{0:T(128)S(1)}, u32[]{:S(2)}) copy-start(f32[128]{0:T(128)S(1)} %convert_element_type.152) | copy-start | bytes 1540
  75.3 128.2 %copy-start.17 = (f32[256,128]{0,1:T(8,128)}, f32[256,128]{0,1:T(8,128)S(1)}, u32[]{:S(2)}) copy-start(f32[256,128]{0,1:T(8,128)S(1)} %get-tuple-element.719) | copy-start | bytes 393220
  75.3 128.2 %copy-start.22 = (f32[256,128]{0,1:T(8,128)}, f32[256,128]{0,1:T(8,128)S(1)}, u32[]{:S(2)}) copy-start(f32[256,128]{0,1:T(8,128)S(1)} %get-tuple-element.718) | copy-start | bytes 393220
  132.2 1.4 copy-start.3
  132.2 1.4 copy-start.40
  132.2 1.4 copy-start.34
  133.7 200.6 %all-gather.20.cloned.1.call-start = ((), (), s32[]{:S(2)}) async-start(), calls=%async_computation.13 | async-start | bytes 4325376 | tf_op jit(solution)/shard_map/all_gather | solution.py:125
  134.3 271.0 %all-gather.24.cloned.1.call-start = ((), (), s32[]{:S(2)}) async-start(), calls=%async_computation.15 | async-start | bytes 6488064 | tf_op jit(solution)/shard_map/all_gather | solution.py:128
  135.0 341.2 %all-gather.22.cloned.1.call-start = ((), (), s32[]{:S(2)}) async-start(), calls=%async_computation.14 | async-start | bytes 6488064 | tf_op jit(solution)/shard_map/all_gather | solution.py:127
  135.8 411.5 %all-gather.26.cloned.1.call-start = ((), (), s32[]{:S(2)}) async-start(), calls=%async_computation.16 | async-start | bytes 6488064 | tf_op jit(solution)/shard_map/all_gather | solution.py:129
  136.5 603.0 %reduce-scatter.9.cloned.1.call-start = ((), (), s32[]{:S(2)}) async-start(), calls=%async_computation.17 | async-start | bytes 9437184 | tf_op jit(solution)/shard_map/reduce_scatter | solution.py:291
  137.1 66.4 %copy-start.46 = (f32[128]{0:T(128)}, f32[128]{0:T(128)S(1)}, u32[]{:S(2)}) copy-start(f32[128]{0:T(128)S(1)} %convert_element_type.156) | copy-start | bytes 1540
  202.8 1.3 copy-start.1
  202.9 1.3 copy-start.30
  270.7 2.0 copy-start
  274.3 1.8 copy-start.19
  281.9 2.0 copy-start
  285.6 1.8 copy-start.19
  293.2 2.0 copy-start
  296.8 1.8 copy-start.19
  304.5 2.0 copy-start
  308.1 1.8 copy-start.19
  547.2 9.2 copy-start.49
  556.4 1.9 copy-start.25
  556.4 1.9 copy-start.26
  556.4 2.0 copy-start.13
  558.4 5.8 copy-start.21
  558.4 7.2 copy-start.50
  669.5 259.8 %reduce-scatter.17.cloned.1.call-start = ((), (), s32[]{:S(2)}) async-start(), calls=%async_computation.21 | async-start | bytes 8650752 | tf_op jit(solution)/shard_map/reduce_scatter | solution.py:313
  677.0 412.8 %reduce-scatter.23.cloned.1.call-start = ((), (), s32[]{:S(2)}) async-start(), calls=%async_computation.24 | async-start | bytes 12976128 | tf_op jit(solution)/shard_map/reduce_scatter | solution.py:317
  686.3 564.7 %reduce-scatter.21.cloned.1.call-start = ((), (), s32[]{:S(2)}) async-start(), calls=%async_computation.23 | async-start | bytes 12976128 | tf_op jit(solution)/shard_map/reduce_scatter | solution.py:316
  694.6 718.4 %reduce-scatter.19.cloned.1.call-start = ((), (), s32[]{:S(2)}) async-start(), calls=%async_computation.22 | async-start | bytes 12976128 | tf_op jit(solution)/shard_map/reduce_scatter | solution.py:315
  702.8 897.8 %reduce-scatter.11.cloned.1.call-start = ((), (), s32[]{:S(2)}) async-start(), calls=%async_computation.18 | async-start | bytes 8650752 | tf_op jit(solution)/shard_map/reduce_scatter | solution.py:308
  703.9 1.6 copy-start.2
  703.9 1.6 copy-start.28
  703.9 1.6 copy-start.31
  703.9 1.6 copy-start.47
  706.6 1.6 copy-start.6
  706.6 1.6 copy-start.33
  706.6 1.6 copy-start.39
  713.0 1035.7 %reduce-scatter.15.cloned.1.call-start = ((), (), s32[]{:S(2)}) async-start(), calls=%async_computation.20 | async-start | bytes 4325376 | tf_op jit(solution)/shard_map/reduce_scatter | solution.py:310
  743.4 2.1 copy-start.4
  743.4 2.1 slice-start
  743.4 2.1 copy-start.18
  743.4 2.1 copy-start.35
  743.4 2.1 copy-start.45
  743.4 1154.2 %reduce-scatter.13.cloned.1.call-start = ((), (), s32[]{:S(2)}) async-start(), calls=%async_computation.19 | async-start | bytes 4325376 | tf_op jit(solution)/shard_map/reduce_scatter | solution.py:309
  743.7 1.9 copy-start.10
  744.3 1.8 copy-start.41
  750.5 3.6 copy-start.14
  750.5 3.7 copy-start.24
  754.2 5.6 copy-start.9
  759.8 1.9 copy-start.51
  761.7 45.6 %copy-start.43 = (f32[256]{0:T(256)S(1)}, f32[256]{0:T(256)}, u32[]{:S(2)}) copy-start(f32[256]{0:T(256)} %copy-done.42) | copy-start | bytes 3076
  (19 other events, 21.6 us)
Sparse Core Ops, SparseCore 0:
  10.9 59.1 all-gather.15
  73.1 55.3 all-gather.9
  131.5 60.9 all-gather.13
  194.2 35.2 all-gather.17
  231.8 37.4 all-gather.11
  272.1 62.0 all-gather.19
  337.1 68.0 all-gather.23
  408.2 68.0 all-gather.21
  479.1 68.0 all-gather.25
  669.7 69.7 reduce-scatter.8
  742.4 186.8 reduce-scatter.16
  936.8 153.0 reduce-scatter.22
  1096.4 154.4 reduce-scatter.20
  1258.5 154.4 reduce-scatter.18
  1415.7 184.9 reduce-scatter.10
  1603.4 145.3 reduce-scatter.14
  1751.4 146.1 reduce-scatter.12
where the time goes:
time: 1910 us; the launch traced here: 1900 us
  waiting for transfers between devices  1510 us (79%)
  matrix products  152 us (8%)
  blocking collectives  84.5 us (4%)
  local copies, waits for them, and re-layouts  77.8 us (4%)
  other arithmetic  60.8 us (3%)
    reduce_scatter x1, waiting for transfers between devices, on_device(): lax.psum_scatter(grad_query, ('ctx', 'fsdp'), scatter_dimension=0, tiled=...  188 us
    reduce_scatter x1, waiting for transfers between devices, on_device(): lax.psum_scatter(grad_gate, ('ctx', 'fsdp'), scatter_dimension=0, tiled=T...  162 us
    reduce_scatter x1, waiting for transfers between devices, on_device(): lax.psum_scatter(grad_up, ('ctx', 'fsdp'), scatter_dimension=0, tiled=True)  161 us
    reduce_scatter x1, waiting for transfers between devices, on_device(): lax.psum_scatter(grad_down, ('ctx', 'fsdp'), scatter_dimension=0, tiled=T...  161 us
    reduce_scatter x1, waiting for transfers between devices, on_device(): lax.psum_scatter(grad_key, ('ctx', 'fsdp'), scatter_dimension=0, tiled=True)  149 us
    reduce_scatter x1, waiting for transfers between devices, on_device(): lax.psum_scatter(grad_value, ('ctx', 'fsdp'), scatter_dimension=0, tiled=...  148 us
    reduce_scatter x1, waiting for transfers between devices, on_device(): lax.psum_scatter(grad_wout, ('ctx', 'fsdp'), scatter_dimension=0, tiled=T...  121 us
    unnamed x2, blocking collectives  84.5 us
  transfers between devices with their start and end apart: 17, of which 17 were waited for; matrix products, arithmetic and copies ran while one was open for 8% of the time, Pallas kernels for 0%

commit v1 on v0

--- a/solution.py
+++ b/solution.py
@@ -1,7 +1,808 @@
+import functools
+import math
+
 import jax
 import jax.numpy as jnp
 from jax import lax
+from jax.experimental import pallas as pl
+from jax.experimental.pallas import tpu as pltpu
 from jax.sharding import PartitionSpec as P
+
+BF = jnp.bfloat16
+F32 = jnp.float32
+MESH = pl.DeviceIdType.MESH
+VMEM = pl.BlockSpec(memory_space=pltpu.VMEM)
+GAIN_ROWS = 24
+LANES = 128
+TILE = 256
+LIMIT = 60 * 2**20
+
+
+def dot(a, b):
+    return jnp.dot(a, b, preferred_element_type=F32)
+
+
+def dot_rt(a, b):
+    return lax.dot_general(a, b, (((1,), (1,)), ((), ())), preferred_element_type=F32)
+
+
+def dot_lt(a, b):
+    return lax.dot_general(a, b, (((0,), (0,)), ((), ())), preferred_element_type=F32)
+
+
+def flip(place, mask, size):
+    out, bit = 0, 1
+    while bit < size:
+        out = out + bit * lax.rem(lax.div(place, bit) + (mask // bit) % 2, 2)
+        bit *= 2
+    return out
+
+
+class Net:
+    def __init__(self, n, nz, send, recv):
+        self.n, self.nz, self.send, self.recv = n, nz, send, recv
+        self.c = lax.axis_index("ctx")
+        self.z = lax.axis_index("fsdp")
+
+    def at(self, mask):
+        return flip(self.c, mask, self.n)
+
+    def zat(self, mask):
+        return flip(self.z, mask, self.nz)
+
+    def peer(self, mask):
+        return (self.at(mask), self.z)
+
+    def zpeer(self, mask):
+        return (self.c, self.zat(mask))
+
+    def barrier(self):
+        bar = pltpu.get_barrier_semaphore()
+        for mask in range(1, self.n):
+            pl.semaphore_signal(bar, inc=1, device_id=self.peer(mask), device_id_type=MESH)
+        for mask in range(1, self.nz):
+            pl.semaphore_signal(bar, inc=1, device_id=self.zpeer(mask), device_id_type=MESH)
+        pl.semaphore_wait(bar, self.n + self.nz - 2)
+
+    def copy(self, src, dst, slot, device):
+        return pltpu.make_async_remote_copy(
+            src_ref=src,
+            dst_ref=dst,
+            send_sem=self.send.at[slot],
+            recv_sem=self.recv.at[slot],
+            device_id=device,
+            device_id_type=MESH,
+        )
+
+
+class Gather:
+    def __init__(self, net, src, buf, base):
+        self.net, self.buf, self.base = net, buf, base
+        self.copies = {}
+        evens = list(range(2, net.n, 2))
+        for mask in [1] + evens[::-1]:
+            cp = net.copy(src, buf.at[net.c], base + mask, net.peer(mask))
+            cp.start()
+            self.copies[mask] = cp
+
+    def arrive(self, mask):
+        net = self.net
+        self.copies[mask].wait_recv()
+        if mask % 2 == 0:
+            d = net.at(mask)
+            cp = net.copy(self.buf.at[d], self.buf.at[d], self.base + mask + 1, net.peer(1))
+            cp.start()
+            self.copies[mask + 1] = cp
+
+    def finish(self):
+        for cp in self.copies.values():
+            cp.wait_send()
+
+
+class PlaneSum:
+    def __init__(self, net, sib_out, sib_in, out, inn, keep, base):
+        self.net, self.base = net, base
+        self.sib_out, self.sib_in, self.out, self.inn, self.keep = sib_out, sib_in, out, inn, keep
+        self.copies = []
+        self.pending = {}
+
+    def give_sibling(self, mask, value):
+        i = mask // 2
+        self.sib_out[i] = value.astype(BF)
+        cp = self.net.copy(self.sib_out.at[i], self.sib_in.at[i], self.base + mask + 1, self.net.peer(1))
+        cp.start()
+        self.copies.append(cp)
+        self.pending[mask] = cp
+
+    def give(self, mask, value):
+        i = mask // 2
+        self.pending[mask].wait_recv()
+        both = value + self.sib_in[i].astype(F32)
+        if mask == 0:
+            self.keep[...] = both
+            return
+        self.out[i - 1] = both.astype(BF)
+        cp = self.net.copy(self.out.at[i - 1], self.inn.at[i - 1], self.base + mask, self.net.peer(mask))
+        cp.start()
+        self.copies.append(cp)
+        self.pending[mask] = cp
+
+    def total(self):
+        for mask in range(2, self.net.n, 2):
+            self.pending[mask].wait_recv()
+        value = self.keep[...]
+        for i in range(self.net.n // 2 - 1):
+            value = value + self.inn[i].astype(F32)
+        return value
+
+    def finish(self):
+        for cp in self.copies:
+            cp.wait_send()
+
+
+def plane_sum_scratch(n, rows, width):
+    half = n // 2
+    return [
+        pltpu.VMEM((half, rows, width), BF),
+        pltpu.VMEM((half, rows, width), BF),
+        pltpu.VMEM((half - 1, rows, width), BF),
+        pltpu.VMEM((half - 1, rows, width), BF),
+        pltpu.VMEM((rows, width), F32),
+    ]
+
+
+def row_of(g, first, count):
+    return jnp.concatenate([g[first + j : first + j + 1, :] for j in range(count)], axis=1)
+
+
+def half_places(net, d, half):
+    per = TILE // half
+    blocks = (d, 2 * net.n - 1 - d)
+    return [(lax.div(b, per), pl.multiple_of(lax.rem(b, per) * half, half)) for b in blocks]
+
+
+def gather_qkv(cfg, x_ref, wqkv_ref, gu_ref, wo_ref, gains_ref, cos_ref, sin_ref,
+               xn_ref, q_ref, k_ref, v_ref, pre_ref, gu_out, wo_out, w_ref, gains_out,
+               xg, gbuf, gz, send, recv):
+    n, nz, ql, kvl, hd = cfg["n"], cfg["nz"], cfg["ql"], cfg["kvl"], cfg["hd"]
+    t, dm = x_ref.shape
+    net = Net(n, nz, send, recv)
+    c, z = net.c, net.z
+    net.barrier()
+    slot = 0
+    plane = []
+    for mask in range(1, n):
+        cp = net.copy(gains_ref, gbuf.at[c], slot + mask, net.peer(mask))
+        cp.start()
+        plane.append(cp)
+    slot += n
+    for mask in range(1, n):
+        cp = net.copy(wqkv_ref.at[net.at(mask)], w_ref.at[c, z], slot + mask, net.peer(mask))
+        cp.start()
+        plane.append(cp)
+    slot += n
+    line = []
+    for mask in range(1, nz):
+        cp = net.copy(wo_ref, wo_out.at[z], slot + mask, net.zpeer(mask))
+        cp.start()
+        line.append(cp)
+    slot += nz
+    gath = Gather(net, x_ref, xg, slot)
+    slot += n
+    late = []
+    for mask in range(1, n):
+        cp = net.copy(gu_ref.at[net.at(mask)], gu_out.at[c], slot + mask, net.peer(mask))
+        cp.start()
+        late.append(cp)
+    slot += n
+    gbuf[c] = gains_ref[...]
+    w_ref[c, z] = wqkv_ref[c]
+    gu_out[c] = gu_ref[c]
+    wo_out[z] = wo_ref[...]
+    xg[c] = x_ref[...]
+    for cp in plane[: n - 1]:
+        cp.wait_recv()
+    gz[z] = jnp.sum(gbuf[...], axis=0)
+    gains_line = []
+    for mask in range(1, nz):
+        cp = net.copy(gz.at[z], gz.at[z], slot + mask, net.zpeer(mask))
+        cp.start()
+        gains_line.append(cp)
+    slot += nz
+    for cp in plane[n - 1 :]:
+        cp.wait_recv()
+    for mask in range(1, nz):
+        cp = net.copy(w_ref.at[:, z], w_ref.at[:, z], slot + mask, net.zpeer(mask))
+        cp.start()
+        line.append(cp)
+    slot += nz
+    for cp in gains_line:
+        cp.wait_recv()
+    gains = jnp.sum(gz[...], axis=0)
+    gains_out[...] = gains
+    g_in = row_of(gains, 0, dm // LANES)
+    g_q = gains[16:17, :]
+    g_k = gains[17:18, :]
+    step = 32
+
+    def normalise(d):
+        def rows(i, carry):
+            at = pl.ds(pl.multiple_of(i * step, step), step)
+            x = xg[d, at, :].astype(F32)
+            r = lax.rsqrt(jnp.mean(x * x, axis=-1, keepdims=True) + cfg["eps"])
+            xn_ref[d, at, :] = (x * r * g_in).astype(BF)
+            return carry
+
+        lax.fori_loop(0, t // step, rows, 0)
+
+    order = [0, 1] + [m for e in range(2, n, 2) for m in (e,)] + [m for e in range(2, n, 2) for m in (e + 1,)]
+    for mask in order:
+        if mask:
+            gath.arrive(mask)
+        normalise(net.at(mask))
+    for cp in line:
+        cp.wait_recv()
+    w = w_ref[...].reshape(dm, -1)
+
+    def head_block(d, carry):
+        qkv = dot(xn_ref[d], w)
+        width = (ql + kvl) * hd
+        pre_ref[d] = qkv[:, :width]
+        cos, sin = cos_ref[d], sin_ref[d]
+        places = half_places(net, d, t // 2)
+        for h in range(ql + kvl):
+            v = qkv[:, h * hd : (h + 1) * hd]
+            r = lax.rsqrt(jnp.mean(v * v, axis=-1, keepdims=True) + cfg["eps"])
+            hat = v * r * (g_q if h < ql else g_k)
+            low = (hat * cos + pltpu.roll(hat, hd // 2, 1) * sin).astype(BF)
+            for s, (tile, row) in enumerate(places):
+                part = low[s * (t // 2) : (s + 1) * (t // 2)]
+                if h < ql:
+                    q_ref[tile, h, pl.ds(row, t // 2), :] = part
+                else:
+                    k_ref[tile, h - ql, pl.ds(row, t // 2), :] = part
+        for h in range(kvl):
+            low = qkv[:, width + h * hd : width + (h + 1) * hd].astype(BF)
+            for s, (tile, row) in enumerate(places):
+                v_ref[tile, h, pl.ds(row, t // 2), :] = low[s * (t // 2) : (s + 1) * (t // 2)]
+        return carry
+
+    lax.fori_loop(0, n, head_block, 0)
+    for cp in late:
+        cp.wait_recv()
+    gath.finish()
+    for cp in plane + line + gains_line + late:
+        cp.wait_send()
+
+
+def attend(cfg, q_ref, k_ref, v_ref, start_ref, db_ref, gu_ref,
+           attn_ref, qx_ref, dblk_ref, gu_out,
+           vx, acc, send, recv):
+    n, nz, ql, hd = cfg["n"], cfg["nz"], cfg["ql"], cfg["hd"]
+    tiles = q_ref.shape[0]
+    net = Net(n, nz, send, recv)
+    c, z = net.c, net.z
+    net.barrier()
+    line = []
+    for mask in range(1, nz):
+        cp = net.copy(gu_ref, gu_out.at[:, z], mask, net.zpeer(mask))
+        cp.start()
+        line.append(cp)
+    gath = Gather(net, db_ref, dblk_ref, nz)
+    gu_out[:, z] = gu_ref[...]
+    dblk_ref[c] = db_ref[...]
+    rows = ql * TILE
+    factor = math.log2(math.e) / math.sqrt(hd)
+    vx[:, :, :hd] = v_ref[:, 0]
+    vx[:, :, hd:] = jnp.ones((tiles, TILE, hd), BF)
+    lane = lax.broadcasted_iota(jnp.int32, (rows, hd), 1)
+
+    def q_tile(i, carry):
+        q = q_ref[i].reshape(rows, hd)
+        start = start_ref[pl.ds(pl.multiple_of(i * TILE, TILE), TILE), :]
+        q_at = i * TILE + lax.broadcasted_iota(jnp.int32, (TILE, TILE), 0)
+        acc[...] = jnp.zeros_like(acc)
+
+        def k_tile(j, carry):
+            s = dot_rt(q, k_ref[j, 0])
+            k_at = j * TILE + lax.broadcasted_iota(jnp.int32, (TILE, TILE), 1)
+            allowed = (k_at <= q_at) & (k_at >= start)
+            e = jnp.where(allowed[None], jnp.exp2(s * factor).reshape(ql, TILE, TILE), 0.0)
+            acc[...] += dot(e.astype(BF).reshape(rows, TILE), vx[j])
+            return carry
+
+        lax.fori_loop(jnp.maximum(i - cfg["window"], 0), i + 1, k_tile, 0)
+        total = acc[:, hd:]
+        attn = acc[:, :hd] / total
+        for h in range(ql):
+            attn_ref[pl.ds(pl.multiple_of(i * TILE, TILE), TILE), h * hd : (h + 1) * hd] = attn[
+                h * TILE : (h + 1) * TILE
+            ].astype(BF)
+        extra = jnp.log(total) * math.sqrt(hd)
+        qx_ref[i, :, :, :hd] = q_ref[i]
+        qx_ref[i, :, :, hd:] = split_three(extra, lane).reshape(ql, TILE, hd)
+        return carry
+
+    lax.fori_loop(0, tiles, q_tile, 0)
+    for mask in list(range(2, n, 2)) + [1] + list(range(3, n, 2)):
+        gath.arrive(mask)
+    for cp in line:
+        cp.wait_recv()
+    gath.finish()
+    for cp in line:
+        cp.wait_send()
+
+
+def split_three(value, lane):
+    first = value.astype(BF).astype(F32)
+    rest = value - first
+    second = rest.astype(BF).astype(F32)
+    third = rest - second
+    out = jnp.where(lane == 0, first, jnp.where(lane == 1, second, jnp.where(lane == 2, third, 0.0)))
+    return out.astype(BF)
+
+
+def feed(cfg, attn_ref, x_ref, dblk_ref, wo_ref, gu_ref, wd_ref, gains_ref,
+         mo_ref, dax_ref, hmid_ref, dhmid_ref, gwo_ref, gwd_ref, ggu_ref, gpost_ref,
+         wd_all, hn, act, dgu, dres, gwd_buf, ggu_buf, gwd_in, ggu_in, *rest):
+    n, nz, ql, hd, ff = cfg["n"], cfg["nz"], cfg["ql"], cfg["hd"], cfg["ff"]
+    first, second, (hres, send, recv) = rest[:5], rest[5:10], rest[10:]
+    t, dm = x_ref.shape
+    half = t // 2
+    net = Net(n, nz, send, recv)
+    c, z = net.c, net.z
+    net.barrier()
+    slot = 0
+    line = []
+    for mask in range(1, nz):
+        cp = net.copy(wd_ref, wd_all.at[z], slot + mask, net.zpeer(mask))
+        cp.start()
+        line.append(cp)
+    slot += nz
+    wd_all[z] = wd_ref[...]
+    wo = wo_ref[...].reshape(-1, dm)
+
+    def attn_rows(d):
+        return jnp.concatenate(
+            [attn_ref[pl.ds(pl.multiple_of(b * half, half), half), :] for b in (d, 2 * n - 1 - d)], axis=0
+        )
+
+    sum1 = PlaneSum(net, *first, slot)
+    slot += n
+    for mask in list(range(2, n, 2))[::-1] + [0]:
+        sum1.give_sibling(mask, dot(attn_rows(net.at(mask + 1)), wo))
+        sum1.give(mask, dot(attn_rows(net.at(mask)), wo))
+    g_post = row_of(gains_ref[...], 8, dm // LANES)
+    h_mid = x_ref[...].astype(F32) + sum1.total()
+    hmid_ref[...] = h_mid
+    r_mid = lax.rsqrt(jnp.mean(h_mid * h_mid, axis=-1, keepdims=True) + cfg["eps"])
+    hres[...] = (h_mid * r_mid * g_post).astype(BF)
+    gath1 = Gather(net, hres, hn, slot)
+    slot += n
+    hn[c] = hres[...]
+    for cp in line:
+        cp.wait_recv()
+    wgu = gu_ref[...].reshape(dm, -1)
+    wd = wd_all[...].reshape(-1, dm)
+
+    def block(d):
+        gu = dot(hn[d], wgu)
+        gate, up = gu[:, :ff], gu[:, ff:]
+        sig = 1.0 / (1.0 + jnp.exp(-gate))
+        silu = gate * sig
+        low = (silu * up).astype(BF)
+        act[d] = low
+        mo_ref[d] = dot(low, wd).astype(BF)
+        d_act = dot_rt(dblk_ref[d], wd)
+        d_gate = (d_act * up * sig * (1.0 + gate * (1.0 - sig))).astype(BF)
+        d_up = (d_act * silu).astype(BF)
+        dgu[d, :, :ff] = d_gate
+        dgu[d, :, ff:] = d_up
+        return dot_rt(dgu[d], wgu)
+
+    sum2 = PlaneSum(net, *second, slot)
+    slot += n
+    for mask in range(0, n, 2):
+        if mask:
+            gath1.arrive(mask)
+            gath1.arrive(mask + 1)
+        else:
+            gath1.arrive(1)
+        sum2.give_sibling(mask, block(net.at(mask + 1)))
+        sum2.give(mask, block(net.at(mask)))
+    rows = n * t
+    dgu_all = dgu[...].reshape(rows, 2 * ff)
+    gwd_buf[...] = dot_lt(act[...].reshape(rows, ff), dblk_ref[...].reshape(rows, dm)).astype(BF).reshape(gwd_buf.shape)
+    gline = []
+    for mask in range(1, nz):
+        cp = net.copy(gwd_buf.at[net.zat(mask)], gwd_in.at[mask - 1], slot + mask, net.zpeer(mask))
+        cp.start()
+        gline.append(cp)
+    slot += nz
+    per = dm // n
+    cols = 2
+    wide = dm // cols
+    for j in range(cols):
+        part = dot_lt(hn[:, :, j * wide : (j + 1) * wide].reshape(rows, wide), dgu_all)
+        ggu_buf[j * (n // cols) : (j + 1) * (n // cols)] = part.astype(BF).reshape(n // cols, nz, per // nz, 2 * ff)
+    for mask in range(1, nz):
+        cp = net.copy(ggu_buf.at[:, net.zat(mask)], ggu_in.at[mask - 1], slot + mask, net.zpeer(mask))
+        cp.start()
+        gline.append(cp)
+    slot += nz
+    d_hn = sum2.total()
+    v = hmid_ref[...]
+    r = lax.rsqrt(jnp.mean(v * v, axis=-1, keepdims=True) + cfg["eps"])
+    gpost_ref[...] = jnp.sum(d_hn * v * r, axis=0, keepdims=True)
+    gdy = g_post * d_hn
+    d_hmid = dblk_ref[c].astype(F32) + r * gdy - v * (r * r * r) * jnp.mean(gdy * v, axis=-1, keepdims=True)
+    dhmid_ref[...] = d_hmid
+    gath1.finish()
+    hres[...] = d_hmid.astype(BF)
+    gath2 = Gather(net, hres, dres, slot)
+    slot += n
+    dres[c] = hres[...]
+    lane = lax.broadcasted_iota(jnp.int32, (half, hd), 1)
+
+    def back(d):
+        d_attn = dot_rt(dres[d], wo)
+        for s, (tile, row) in enumerate(half_places(net, d, half)):
+            b = (d, 2 * n - 1 - d)[s]
+            attn = attn_ref[pl.ds(pl.multiple_of(b * half, half), half), :].astype(F32)
+            low = d_attn[s * half : (s + 1) * half].astype(BF)
+            prod = low.astype(F32) * attn
+            for h in range(ql):
+                delta = jnp.sum(prod[:, h * hd : (h + 1) * hd], axis=-1, keepdims=True)
+                dax_ref[tile, h, pl.ds(row, half), :hd] = low[:, h * hd : (h + 1) * hd]
+                dax_ref[tile, h, pl.ds(row, half), hd:] = split_three(jnp.broadcast_to(delta, (half, hd)), lane)
+
+    back(c)
+    for mask in [1] + list(range(2, n, 2)) + list(range(3, n, 2)):
+        gath2.arrive(mask)
+        back(net.at(mask))
+    total = None
+    for s in range(2):
+        blocks = attn_ref[s * (rows // 2) : (s + 1) * (rows // 2), :]
+        if s:
+            blocks = jnp.concatenate([blocks[(n - 1 - i) * half : (n - i) * half] for i in range(n)], axis=0)
+        part = dot_lt(blocks, dres[:, s * half : (s + 1) * half, :].reshape(n * half, dm))
+        total = part if total is None else total + part
+    gwo_ref[...] = total.astype(BF).reshape(gwo_ref.shape)
+    for cp in gline:
+        cp.wait_recv()
+    gwd = gwd_buf[z].astype(F32)
+    ggu = ggu_buf[:, z].astype(F32)
+    for i in range(nz - 1):
+        gwd = gwd + gwd_in[i].astype(F32)
+        ggu = ggu + ggu_in[i].astype(F32)
+    gwd_ref[...] = gwd
+    ggu_ref[...] = ggu.astype(BF)
+    for part in (sum1, sum2, gath2):
+        part.finish()
+    for cp in line + gline:
+        cp.wait_send()
+
+
+def attend_back(cfg, qx_ref, k_ref, v_ref, dax_ref, start_ref, mo_ref, hmid_ref, valid_ref, gwo_ref, ggu_ref,
+                dq_ref, dk_ref, dv_ref, block_ref, gwo_out, ggate_ref, gup_ref,
+                kx, vx, dk_acc, dv_acc, gwo_in, ggu_in, *rest):
+    n, nz, ql, hd, ff = cfg["n"], cfg["nz"], cfg["ql"], cfg["hd"], cfg["ff"]
+    sums, (send, recv) = rest[:5], rest[5:]
+    tiles = qx_ref.shape[0]
+    net = Net(n, nz, send, recv)
+    c, z = net.c, net.z
+    net.barrier()
+    slot = 0
+    sum1 = PlaneSum(net, *sums, slot)
+    slot += n
+    for mask in list(range(2, n, 2))[::-1] + [0]:
+        sum1.give_sibling(mask, mo_ref[net.at(mask + 1)])
+    for mask in list(range(2, n, 2))[::-1] + [0]:
+        sum1.give(mask, mo_ref[net.at(mask)].astype(F32))
+    line = []
+    for mask in range(1, nz):
+        cp = net.copy(gwo_ref.at[net.zat(mask)], gwo_in.at[mask - 1], slot + mask, net.zpeer(mask))
+        cp.start()
+        line.append(cp)
+    slot += nz
+    for mask in range(1, n):
+        cp = net.copy(ggu_ref.at[net.at(mask)], ggu_in.at[c], slot + mask, net.peer(mask))
+        cp.start()
+        line.append(cp)
+    slot += n
+    ggu_in[c] = ggu_ref[c]
+    rows = ql * TILE
+    factor = math.log2(math.e) / math.sqrt(hd)
+    scale = 1.0 / math.sqrt(hd)
+    lane = lax.broadcasted_iota(jnp.int32, (tiles, TILE, hd), 2)
+    minus = jnp.where(lane < 3, -1.0, 0.0).astype(BF)
+    kx[:, :, :hd] = k_ref[:, 0]
+    kx[:, :, hd:] = minus
+    vx[:, :, :hd] = v_ref[:, 0]
+    vx[:, :, hd:] = minus
+    dq_ref[...] = jnp.zeros_like(dq_ref)
+
+    def k_tile(j, carry):
+        k_at = j * TILE + lax.broadcasted_iota(jnp.int32, (TILE, TILE), 0)
+        dk_acc[...] = jnp.zeros_like(dk_acc)
+        dv_acc[...] = jnp.zeros_like(dv_acc)
+
+        def q_tile(i, carry):
+            qx = qx_ref[i].reshape(rows, 2 * hd)
+            dax = dax_ref[i].reshape(rows, 2 * hd)
+            start = start_ref[:, pl.ds(pl.multiple_of(i * TILE, TILE), TILE)]
+            q_at = i * TILE + lax.broadcasted_iota(jnp.int32, (TILE, TILE), 1)
+            allowed = (k_at <= q_at) & (k_at >= start)
+            allowed = jnp.concatenate([allowed] * ql, axis=1)
+            s = dot_rt(kx[j], qx)
+            p = jnp.where(allowed, jnp.exp2(s * factor), 0.0)
+            ds = (p * dot_rt(vx[j], dax)).astype(BF)
+            dv_acc[...] += dot(p.astype(BF), dax[:, :hd])
+            dk_acc[...] += dot(ds, qx[:, :hd])
+            dq_ref[i] += dot_lt(ds, k_ref[j, 0])
+            return carry
+
+        lax.fori_loop(j, jnp.minimum(j + cfg["window"], tiles - 1) + 1, q_tile, 0)
+        dk_ref[j] = dk_acc[...] * scale
+        dv_ref[j] = dv_acc[...]
+        return carry
+
+    lax.fori_loop(0, tiles, k_tile, 0)
+    dq_ref[...] = dq_ref[...] * scale
+    for cp in line:
+        cp.wait_recv()
+    gwo = gwo_ref[z].astype(F32)
+    for i in range(nz - 1):
+        gwo = gwo + gwo_in[i].astype(F32)
+    gwo_out[...] = gwo
+    for d in range(n):
+        both = ggu_in[d].astype(F32)
+        ggate_ref[:, d * ff : (d + 1) * ff] = both[:, :ff]
+        gup_ref[:, d * ff : (d + 1) * ff] = both[:, ff:]
+    block_ref[...] = (valid_ref[...] * (hmid_ref[...] + sum1.total())).astype(BF)
+    sum1.finish()
+    for cp in line:
+        cp.wait_send()
+
+
+def head_back(cfg, pre_ref, dq_ref, dk_ref, dv_ref, cos_ref, sin_ref, gains_ref, xn_ref, w_ref, x_ref, dhmid_ref,
+              gpost_ref,
+              dx_ref, gq_ref, gk_ref, gv_ref, gains_out,
+              dqkv, gbuf, g_in_line, gsum, g_in, part, gplane, gz, *rest):
+    n, nz, ql, kvl, hd = cfg["n"], cfg["nz"], cfg["ql"], cfg["kvl"], cfg["hd"]
+    sums, (send, recv) = rest[:5], rest[5:]
+    t, dm = x_ref.shape
+    half = t // 2
+    net = Net(n, nz, send, recv)
+    c, z = net.c, net.z
+    net.barrier()
+    gains = gains_ref[...]
+    w = w_ref[...].reshape(dm, -1)
+
+    def head_block(d, carry):
+        pre = pre_ref[d]
+        cos, sin = cos_ref[d], sin_ref[d]
+        places = half_places(net, d, half)
+        new = []
+        for h in range(ql + kvl):
+            if h < ql:
+                dy = jnp.concatenate([dq_ref[tile, pl.ds(h * TILE + row, half), :] for tile, row in places], axis=0)
+            else:
+                dy = jnp.concatenate([dk_ref[tile, pl.ds(row, half), :] for tile, row in places], axis=0)
+            g = gains[16:17, :] if h < ql else gains[17:18, :]
+            v = pre[:, h * hd : (h + 1) * hd]
+            r = lax.rsqrt(jnp.mean(v * v, axis=-1, keepdims=True) + cfg["eps"])
+            dy = dy * cos - pltpu.roll(dy, hd // 2, 1) * sin
+            new.append(jnp.sum(dy * v * r, axis=0, keepdims=True))
+            gdy = g * dy
+            dv = r * gdy - v * (r * r * r) * jnp.mean(gdy * v, axis=-1, keepdims=True)
+            dqkv[d, :, h * hd : (h + 1) * hd] = dv.astype(BF)
+        dv = jnp.concatenate([dv_ref[tile, pl.ds(row, half), :] for tile, row in places], axis=0)
+        dqkv[d, :, (ql + kvl) * hd :] = dv.astype(BF)
+        q_sum = sum(new[1:ql], new[0])
+        k_sum = sum(new[ql + 1 :], new[ql])
+        return (carry[0] + q_sum, carry[1] + k_sum)
+
+    zero = jnp.zeros((1, hd), F32)
+    gq, gk = lax.fori_loop(0, n, head_block, (zero, zero))
+    rows = n * t
+    per = dm // n
+    cols = 2
+    wide = dm // cols
+    d_all = dqkv[...].reshape(rows, -1)
+    for j in range(cols):
+        grad = dot_lt(xn_ref[:, :, j * wide : (j + 1) * wide].reshape(rows, wide), d_all)
+        gbuf[j * (n // cols) : (j + 1) * (n // cols)] = grad.astype(BF).reshape(n // cols, nz, per // nz, -1)
+    slot = 0
+    line = []
+    for mask in range(1, nz):
+        cp = net.copy(gbuf.at[:, net.zat(mask)], g_in_line.at[mask - 1], slot + mask, net.zpeer(mask))
+        cp.start()
+        line.append(cp)
+    slot += nz
+    sum1 = PlaneSum(net, *sums, slot)
+    slot += n
+    for mask in list(range(2, n, 2))[::-1] + [0]:
+        sum1.give_sibling(mask, dot_rt(dqkv[net.at(mask + 1)], w))
+        sum1.give(mask, dot_rt(dqkv[net.at(mask)], w))
+    for cp in line:
+        cp.wait_recv()
+    total = gbuf[:, z].astype(F32)
+    for i in range(nz - 1):
+        total = total + g_in_line[i].astype(F32)
+    gsum[...] = total.astype(BF)
+    plane = []
+    for mask in range(1, n):
+        cp = net.copy(gsum.at[net.at(mask)], g_in.at[c], slot + mask, net.peer(mask))
+        cp.start()
+        plane.append(cp)
+    slot += n
+    g_in[c] = gsum[c]
+    d_xn = sum1.total()
+    x = x_ref[...].astype(F32)
+    g = row_of(gains, 0, dm // LANES)
+    r = lax.rsqrt(jnp.mean(x * x, axis=-1, keepdims=True) + cfg["eps"])
+    grad_in = jnp.sum(d_xn * x * r, axis=0, keepdims=True)
+    gdy = g * d_xn
+    dx_ref[...] = dhmid_ref[...] + r * gdy - x * (r * r * r) * jnp.mean(gdy * x, axis=-1, keepdims=True)
+    part[...] = jnp.zeros_like(part)
+    for j in range(dm // LANES):
+        part[j : j + 1, :] = grad_in[:, j * LANES : (j + 1) * LANES]
+        part[8 + j : 9 + j, :] = gpost_ref[:, j * LANES : (j + 1) * LANES]
+    part[16:17, :] = gq
+    part[17:18, :] = gk
+    small = []
+    for mask in range(1, n):
+        cp = net.copy(part, gplane.at[c], slot + mask, net.peer(mask))
+        cp.start()
+        small.append(cp)
+    slot += n
+    gplane[c] = part[...]
+    for cp in small:
+        cp.wait_recv()
+    gz[z] = jnp.sum(gplane[...], axis=0)
+    last = []
+    for mask in range(1, nz):
+        cp = net.copy(gz.at[z], gz.at[z], slot + mask, net.zpeer(mask))
+        cp.start()
+        last.append(cp)
+    for cp in plane:
+        cp.wait_recv()
+    qw, kw = ql * hd, kvl * hd
+    for d in range(n):
+        both = g_in[d].astype(F32)
+        gq_ref[:, d * qw : (d + 1) * qw] = both[:, :qw]
+        gk_ref[:, d * kw : (d + 1) * kw] = both[:, qw : qw + kw]
+        gv_ref[:, d * kw : (d + 1) * kw] = both[:, qw + kw :]
+    for cp in last:
+        cp.wait_recv()
+    gains_out[...] = jnp.sum(gz[...], axis=0)
+    sum1.finish()
+    for cp in line + plane + small + last:
+        cp.wait_send()
+
+
+def call(body, cfg, outs, scratch, cid, *args):
+    slots = cfg["slots"]
+    return pl.pallas_call(
+        functools.partial(body, cfg),
+        out_shape=[jax.ShapeDtypeStruct(shape, dtype) for shape, dtype in outs],
+        in_specs=[VMEM] * len(args),
+        out_specs=[VMEM] * len(outs),
+        scratch_shapes=scratch + [pltpu.SemaphoreType.DMA((slots,)), pltpu.SemaphoreType.DMA((slots,))],
+        compiler_params=pltpu.CompilerParams(collective_id=cid, has_side_effects=True, vmem_limit_bytes=LIMIT),
+        name=body.__name__,
+    )(*args)
+
+
+def rope_base_tables(pos, hd):
+    half = hd // 2
+    inv = jnp.power(1000000.0, -jnp.arange(half, dtype=F32) * (2.0 / hd))
+    angles = pos.astype(F32)[:, None] * inv[None, :]
+    cos, sin = jnp.cos(angles), jnp.sin(angles)
+    return jnp.concatenate([cos, cos], axis=1), jnp.concatenate([-sin, sin], axis=1)
+
+
+def on_plane(hidden_in, seq_lengths, in_gain, w_query, w_key, w_value, q_gain, k_gain, w_out, post_gain,
+             w_gate, w_up, w_down, d_out):
+    n, nz = lax.axis_size("ctx"), lax.axis_size("fsdp")
+    c, z = lax.axis_index("ctx"), lax.axis_index("fsdp")
+    t, dm = hidden_in.shape[1:]
+    half = t // 2
+    rows = n * t
+    hd = q_gain.shape[0] * n * nz
+    ql = w_query.shape[1] // hd // n
+    kvl = w_key.shape[1] // hd // n
+    ff = w_gate.shape[1] // n
+    r_in, r_out, r_down = w_query.shape[0], w_out.shape[0], w_down.shape[0]
+    qkv = (ql + 2 * kvl) * hd
+    tiles = rows // TILE
+    cfg = dict(n=n, nz=nz, ql=ql, kvl=kvl, hd=hd, ff=ff, eps=1e-6, window=rows // 2 // TILE, slots=6 * n + 6 * nz)
+
+    lengths = seq_lengths[0]
+    ends = jnp.cumsum(lengths)
+    begins = ends - lengths
+    packed = jnp.arange(rows, dtype=jnp.int32)
+    inside = packed[:, None] >= begins[None, :]
+    start = jnp.max(jnp.where(inside, begins[None, :], 0), axis=1)
+    start = jnp.where(packed < ends[-1], start, packed).astype(jnp.int32)
+    pos = packed - start
+    by_block = pos.reshape(2 * n, half)
+    pos_dev = jnp.concatenate([by_block[:n, None], by_block[n:][::-1][:, None]], axis=1).reshape(rows)
+    cos, sin = rope_base_tables(pos_dev, hd)
+    cos, sin = cos.reshape(n, t, hd), sin.reshape(n, t, hd)
+    own = jnp.concatenate([c * half + jnp.arange(half), (2 * n - 1 - c) * half + jnp.arange(half)])
+    valid = (own < ends[-1]).astype(F32)[:, None]
+    db = d_out[0] * valid.astype(BF)
+    x = hidden_in[0]
+
+    def place(gain, width):
+        wide = jnp.zeros((width,), F32)
+        return lax.dynamic_update_slice(wide, gain.astype(F32), ((c * nz + z) * gain.shape[0],)).reshape(-1, LANES)
+
+    gains = jnp.concatenate([place(in_gain, dm), place(post_gain, dm), place(q_gain, hd), place(k_gain, hd),
+                             jnp.zeros((GAIN_ROWS - 18, LANES), F32)], axis=0)
+
+    def by_device(w):
+        return jnp.transpose(w.reshape(w.shape[0], n, -1), (1, 0, 2))
+
+    wqkv = jnp.concatenate([by_device(w_query), by_device(w_key), by_device(w_value)], axis=2)
+    wgu = jnp.concatenate([by_device(w_gate), by_device(w_up)], axis=2)
+
+    xn, q, k, v, pre, gu_plane, wo, w, gains = call(
+        gather_qkv, cfg,
+        [((n, t, dm), BF), ((tiles, ql, TILE, hd), BF), ((tiles, kvl, TILE, hd), BF), ((tiles, kvl, TILE, hd), BF),
+         ((n, t, (ql + kvl) * hd), F32), ((n, r_in, 2 * ff), BF), ((nz, r_out, dm), BF), ((n, nz, r_in, qkv), BF),
+         ((GAIN_ROWS, LANES), F32)],
+        [pltpu.VMEM((n, t, dm), BF), pltpu.VMEM((n, GAIN_ROWS, LANES), F32), pltpu.VMEM((nz, GAIN_ROWS, LANES), F32)],
+        1, x, wqkv, wgu, w_out, gains, cos, sin)
+
+    attn, qx, dblk, gu = call(
+        attend, cfg,
+        [((rows, ql * hd), BF), ((tiles, ql, TILE, 2 * hd), BF), ((n, t, dm), BF), ((n, nz, r_in, 2 * ff), BF)],
+        [pltpu.VMEM((tiles, TILE, 2 * hd), BF), pltpu.VMEM((ql * TILE, 2 * hd), F32)],
+        2, q, k, v, start[:, None], db, gu_plane)
+
+    mo, dax, h_mid, d_hmid, gwo, gwd, ggu, gpost = call(
+        feed, cfg,
+        [((n, t, dm), BF), ((tiles, ql, TILE, 2 * hd), BF), ((t, dm), F32), ((t, dm), F32), ((nz, r_out, dm), BF),
+         ((r_down, dm), F32), ((n, r_in, 2 * ff), BF), ((1, dm), F32)],
+        [pltpu.VMEM((nz, r_down, dm), BF), pltpu.VMEM((n, t, dm), BF), pltpu.VMEM((n, t, ff), BF),
+         pltpu.VMEM((n, t, 2 * ff), BF), pltpu.VMEM((n, t, dm), BF),
+         pltpu.VMEM((nz, r_down, dm), BF), pltpu.VMEM((n, nz, r_in, 2 * ff), BF),
+         pltpu.VMEM((nz - 1, r_down, dm), BF), pltpu.VMEM((nz - 1, n, r_in, 2 * ff), BF)]
+        + plane_sum_scratch(n, t, dm) + plane_sum_scratch(n, t, dm) + [pltpu.VMEM((t, dm), BF)],
+        3, attn, x, dblk, wo, gu, w_down, gains)
+
+    dq, dk, dv, block_out, grad_wo, grad_gate, grad_up = call(
+        attend_back, cfg,
+        [((tiles, ql * TILE, hd), F32), ((tiles, TILE, hd), F32), ((tiles, TILE, hd), F32), ((t, dm), BF),
+         ((r_out, dm), F32), ((r_in, n * ff), F32), ((r_in, n * ff), F32)],
+        [pltpu.VMEM((tiles, TILE, 2 * hd), BF), pltpu.VMEM((tiles, TILE, 2 * hd), BF),
+         pltpu.VMEM((TILE, hd), F32), pltpu.VMEM((TILE, hd), F32),
+         pltpu.VMEM((nz - 1, r_out, dm), BF), pltpu.VMEM((n, r_in, 2 * ff), BF)]
+        + plane_sum_scratch(n, t, dm),
+        4, qx, k, v, dax, start[None, :], mo, h_mid, valid, gwo, ggu)
+
+    dx, grad_q, grad_k, grad_v, small = call(
+        head_back, cfg,
+        [((t, dm), F32), ((r_in, n * ql * hd), F32), ((r_in, n * kvl * hd), F32), ((r_in, n * kvl * hd), F32),
+         ((GAIN_ROWS, LANES), F32)],
+        [pltpu.VMEM((n, t, qkv), BF), pltpu.VMEM((n, nz, r_in, qkv), BF), pltpu.VMEM((nz - 1, n, r_in, qkv), BF),
+         pltpu.VMEM((n, r_in, qkv), BF), pltpu.VMEM((n, r_in, qkv), BF),
+         pltpu.VMEM((GAIN_ROWS, LANES), F32), pltpu.VMEM((n, GAIN_ROWS, LANES), F32),
+         pltpu.VMEM((nz, GAIN_ROWS, LANES), F32)]
+        + plane_sum_scratch(n, t, dm),
+        5, pre, dq, dk, dv, cos, sin, gains, xn, w, x, d_hmid, gpost)
+
+    def mine(first, width, share):
+        flat = small[first : first + width // LANES].reshape(width)
+        return lax.dynamic_slice(flat, ((c * nz + z) * share,), (share,))
+
+    return (block_out[None], dx[None], mine(0, dm, in_gain.shape[0]), grad_q, grad_k, grad_v,
+            mine(16, hd, q_gain.shape[0]), mine(17, hd, k_gain.shape[0]), grad_wo,
+            mine(8, dm, post_gain.shape[0]), grad_gate, grad_up, gwd)
+
 
 epsilon = 1e-06
 rope_base = 1000000.0
@@ -81,7 +882,7 @@
     return key_count
 
 
-def on_device(
+def on_rows(
     hidden_in,
     seq_lengths,
     in_gain,
@@ -333,6 +1134,17 @@
     )
 
 
+def on_device(*args):
+    n = lax.axis_size("ctx")
+    hidden_in, w_key, w_out, w_gate, q_gain = args[0], args[4], args[8], args[10], args[6]
+    hd = q_gain.shape[0] * n * lax.axis_size("fsdp")
+    heads, ff = w_key.shape[1] // hd, w_gate.shape[1] // n
+    even = heads % n == 0 and ff % LANES == 0 and w_key.shape[0] % 16 == 0 and w_out.shape[0] % 16 == 0
+    if even and heads == n and (hidden_in.shape[1] * n) % (2 * TILE) == 0:
+        return on_plane(*args)
+    return on_rows(*args)
+
+
 def solution(mesh):
     in_specs = (
         P("fsdp", "ctx", None),

time: 1910 us -> 376 us (0.20)
  waiting for transfers between devices: 1510 us -> 0 us
  Pallas kernels: 0 us -> 331 us
  matrix products: 152 us -> 0 us
  blocking collectives: 84.5 us -> 0 us
  local copies, waits for them, and re-layouts: 77.8 us -> 19.3 us
  other arithmetic: 60.8 us -> 18.1 us
    reduce_scatter x8 -> x0, waiting for transfers between devices: 1120 us -> none  [the longest x1 188 us: on_device(): lax.psum_scatter(grad_query, ('ctx', 'fsdp'), scatter_dimension=0, tiled=...]
    all_gather x9 -> x0, waiting for transfers between devices: 387 us -> none  [the longest x1 65.1 us: on_device(): lax.all_gather(shards[9], ('ctx', 'fsdp'), axis=0, tiled=True)]
    pallas_call x0 -> x5, Pallas kernels: none -> 331 us  [call(): pl.pallas_call(functools.partial(body, cfg), out_shape=[jax.ShapeDtypeStr...]
    dot_general x49 -> x0, matrix products: 152 us -> none  [the longest x7 43.3 us: inner(): lax.dot_general(left, right, (((0,), (0,)), ((), ())), preferred_element_...]
    unnamed x2 -> x0, blocking collectives: 84.5 us -> none
    unnamed x114 -> x29, local copies, waits for them, and re-layouts: 31 us -> 8.93 us
    dynamic_update_slice x4 -> x2, other arithmetic: 20.8 us -> 1.48 us  [place(): lax.dynamic_update_slice(wide, gain.astype(F32), ((c * nz + z) * gain.sha...]
  transfers between devices with their start and end apart: 17 -> 0, of which waited for: 17 -> 0; matrix products, arithmetic and copies ran while one was open for 8% -> 0% of each run, Pallas kernels for 0% -> 0%
where the time goes in v1:
time: 376 us; the launch traced here: 369 us
  Pallas kernels  331 us (88%)
  local copies, waits for them, and re-layouts  19.3 us (5%)
  other arithmetic  18.1 us (5%)
    pallas_call x5, Pallas kernels, call(): pl.pallas_call(functools.partial(body, cfg), out_shape=[jax.ShapeDtypeStr...  331 us
    unnamed x29, local copies, waits for them, and re-layouts  8.93 us

profile of v1, /device:TPU:0, one launch (start us, length us, event | category | flops | bytes accessed | tf_op | source)
XLA Modules:
  0.0 369.4 jit_solution(6855295484950017412)
XLA Ops:
  0.6 0.0 copy-start
  0.7 0.8 copy-done
  1.5 0.9 bitcast_bitcast_fusion.3
  2.4 0.9 copy.70
  3.3 0.7 pad_maximum_fusion.3.wqkv_ref
  4.0 1.1 bitcast_bitcast_fusion
  5.1 0.8 pad_maximum_fusion.2.gu_ref
  5.9 0.7 convert_dynamic-update-slice_fusion.1
  6.6 0.7 convert_dynamic-update-slice_fusion
  7.3 0.7 bitcast_convert_fusion.1
  8.0 0.1 dynamic_update_slice.16
  8.1 0.7 bitcast_convert_fusion
  8.7 0.1 dynamic_update_slice.17
  8.8 1.8 concatenate.41.gains_ref
  10.6 0.8 reduce-window.4
  11.5 0.7 fusion.5
  12.1 0.1 select_reduce_fusion
  12.2 0.6 slice.27
  12.8 0.7 fusion.3
  13.5 0.7 fusion.2
  14.2 3.7 %fusion = (f32[8,256,64]{2,1,0:T(8,128)S(1)}, f32[8,256,64]{2,1,0:T(8,128)S(1)}, f32[8,256,64]{2,1,0:T(8,128)S(1)}) fusion(f32[64]{0:T(128)S(1)} %multiply_power_fusion, f32[8,256]{1,0:T(8,128)S(1)} %fusion.1), kind=kLoop, calls=%fused_computation.8 | loop fusion | flops 262144 | bytes 1581312 | tf_op jit(solution)/shard_map/neg | solution.py:703
  17.9 2.0 pad_maximum_fusion
  19.8 53.0 %gather_qkv.1 = (bf16[8,256,1024]{2,1,0:T(8,128)(2,1)}, bf16[8,2,256,128]{3,2,1,0:T(8,128)(2,1)}, bf16[8,1,256,128]{3,2,1,0:T(8,128)(2,1)}, bf16[8,1,256,128]{3,...) custom-call(bf16[256,1024]{1,0:T(8,128)(2,1)} %bitcast.71, ...), custom_call_target="tpu_custom_call" | custom-call | tf_op jit(solution)/shard_map/gather_qkv/pallas_call | solution.py:687
  72.9 0.4 copy.58
  73.2 1.7 iota_select_fusion.start_ref
  74.9 0.7 fusion.4
  75.6 0.0 copy-done.2
  75.6 0.9 bitcast_multiply_fusion.db_ref
  76.5 42.3 %attend.1 = (bf16[2048,256]{1,0:T(8,128)(2,1)}, bf16[8,2,256,256]{3,2,1,0:T(8,128)(2,1)}, bf16[8,256,1024]{2,1,0:T(8,128)(2,1)}, bf16[8,4,32,768]{3,2,1,0:T(8,128)(2,1)}) custom-call(bf16[8,2,256,128]{3,2,1,0:T(8,128)(2,1)} %get-tuple-element.46.q_ref, bf16[8,1,256,128]{3,2,1,0:T(8,128)(2,1)} %get-tuple-element.47.k_ref, ...), custom_call_target="tpu_custom_call" | custom-call | tf_op jit(solution)/shard_map/attend/pallas_call | solution.py:687
  118.8 134.6 %feed.1 = (bf16[8,256,1024]{2,1,0:T(8,128)(2,1)}, bf16[8,2,256,256]{3,2,1,0:T(8,128)(2,1)}, f32[256,1024]{1,0:T(8,128)}, f32[256,1024]{1,0:T(8,128)}, bf16[4,64,...) custom-call(bf16[2048,256]{1,0:T(8,128)(2,1)} %get-tuple-element.51.attn_ref, ...), custom_call_target="tpu_custom_call" | custom-call | tf_op jit(solution)/shard_map/feed/pallas_call | solution.py:687
  253.4 1.3 compare_select_fusion.start_ref
  254.7 0.6 compare_convert_fusion
  255.3 0.8 copy.59.valid_ref
  256.1 48.6 %attend_back.1 = (f32[8,512,128]{2,1,0:T(8,128)}, f32[8,256,128]{2,1,0:T(8,128)}, f32[8,256,128]{2,1,0:T(8,128)}, bf16[256,1024]{1,0:T(8,128)(2,1)}, f32[64,1024...) custom-call(bf16[8,2,256,256]{3,2,1,0:T(8,128)(2,1)} %get-tuple-element.50.qx_ref, ...), custom_call_target="tpu_custom_call" | custom-call | tf_op jit(solution)/shard_map/attend_back/pallas_call | solution.py:687
  304.8 0.0 copy-start.1
  304.8 52.2 %head_back.1 = (f32[256,1024]{1,0:T(8,128)}, f32[32,2048]{1,0:T(8,128)}, f32[32,1024]{1,0:T(8,128)}, f32[32,1024]{1,0:T(8,128)}, f32[24,128]{1,0:T(8,128)}) custom-call(f32[8,256,384]{2,1,0:T(8,128)} %get-tuple-element.62.pre_ref, f32[8,512,128]{2,1,0:T(8,128)} %get-tuple-element.63.dq_ref, f32[8,256,128]{2,1,0:T(8,128)} %get-tuple-element.64.dk_ref, ...), custom_call_target="tpu_custom_call" | custom-call | tf_op jit(solution)/shard_map/head_back/pallas_call | solution.py:687
  356.9 0.0 copy-start.7
  357.0 0.0 copy-start.9
  357.0 0.0 copy-start.8
  357.0 0.0 copy-start.6
  357.0 0.0 copy-start.5
  357.0 0.0 copy-start.4
  357.0 0.8 slice_bitcast_fusion
  357.8 0.6 dynamic_slice.16
  358.4 0.8 fusion.8
  359.1 0.6 dynamic-slice_bitcast_fusion.1
  359.7 0.6 dynamic-slice_bitcast_fusion
  360.3 0.6 dynamic_slice.21
  360.9 0.0 copy-done.1
  360.9 0.8 copy.84
  361.7 2.3 copy.85
  364.0 0.0 copy-done.7
  364.0 0.7 copy.86
  364.7 0.0 copy-done.9
  364.7 0.7 copy.87
  365.4 0.0 copy-done.8
  365.4 0.7 copy.88
  366.0 0.0 copy-done.6
  366.0 0.7 copy.89
  366.7 0.0 copy-done.5
  366.7 0.7 copy.90
  367.5 0.7 copy.91
  368.2 0.0 copy-done.3
  368.2 0.7 copy.92
  (13 shorter events, 0.0 us)
Async XLA Ops:
  0.6 0.8 copy-start
  19.8 55.8 %copy-start.2 = (bf16[1,256,1024]{2,1,0:T(8,128)(2,1)S(1)}, bf16[1,256,1024]{2,1,0:T(8,128)(2,1)}, u32[]{:S(2)}) copy-start(bf16[1,256,1024]{2,1,0:T(8,128)(2,1)} %param.27) | copy-start | bytes 1572868
  304.8 56.1 %copy-start.1 = (bf16[256,1024]{1,0:T(8,128)(2,1)S(1)}, bf16[256,1024]{1,0:T(8,128)(2,1)}, u32[]{:S(2)}) copy-start(bf16[256,1024]{1,0:T(8,128)(2,1)} %get-tuple-element.61) | copy-start | bytes 1572868
  356.9 7.0 %copy-start.7 = (f32[32,2048]{1,0:T(8,128)S(1)}, f32[32,2048]{1,0:T(8,128)}, u32[]{:S(2)}) copy-start(f32[32,2048]{1,0:T(8,128)} %get-tuple-element.112) | copy-start | bytes 786436
  357.0 7.7 %copy-start.9 = (f32[32,1024]{1,0:T(8,128)S(1)}, f32[32,1024]{1,0:T(8,128)}, u32[]{:S(2)}) copy-start(f32[32,1024]{1,0:T(8,128)} %get-tuple-element.113) | copy-start | bytes 393220
  357.0 8.4 %copy-start.8 = (f32[32,1024]{1,0:T(8,128)S(1)}, f32[32,1024]{1,0:T(8,128)}, u32[]{:S(2)}) copy-start(f32[32,1024]{1,0:T(8,128)} %get-tuple-element.114) | copy-start | bytes 393220
  357.0 9.0 %copy-start.6 = (f32[64,1024]{1,0:T(8,128)S(1)}, f32[64,1024]{1,0:T(8,128)}, u32[]{:S(2)}) copy-start(f32[64,1024]{1,0:T(8,128)} %get-tuple-element.117) | copy-start | bytes 786436
  357.0 9.7 %copy-start.5 = (f32[32,3072]{1,0:T(8,128)S(1)}, f32[32,3072]{1,0:T(8,128)}, u32[]{:S(2)}) copy-start(f32[32,3072]{1,0:T(8,128)} %get-tuple-element.119) | copy-start | bytes 1179652
  357.0 10.5 %copy-start.4 = (f32[32,3072]{1,0:T(8,128)S(1)}, f32[32,3072]{1,0:T(8,128)}, u32[]{:S(2)}) copy-start(f32[32,3072]{1,0:T(8,128)} %get-tuple-element.120) | copy-start | bytes 1179652
  360.9 7.3 %copy-start.3 = (f32[96,1024]{1,0:T(8,128)S(1)}, f32[96,1024]{1,0:T(8,128)}, u32[]{:S(2)}) copy-start(f32[96,1024]{1,0:T(8,128)} %get-tuple-element.121) | copy-start | bytes 1179652

commit v2 on v1

--- a/solution.py
+++ b/solution.py
@@ -3,6 +3,7 @@
 
 import jax
 import jax.numpy as jnp
+import numpy as np
 from jax import lax
 from jax.experimental import pallas as pl
 from jax.experimental.pallas import tpu as pltpu
@@ -161,44 +162,99 @@
     return [(lax.div(b, per), pl.multiple_of(lax.rem(b, per) * half, half)) for b in blocks]
 
 
-def gather_qkv(cfg, x_ref, wqkv_ref, gu_ref, wo_ref, gains_ref, cos_ref, sin_ref,
-               xn_ref, q_ref, k_ref, v_ref, pre_ref, gu_out, wo_out, w_ref, gains_out,
-               xg, gbuf, gz, send, recv):
-    n, nz, ql, kvl, hd = cfg["n"], cfg["nz"], cfg["ql"], cfg["kvl"], cfg["hd"]
+def split_three(value, lane):
+    first = value.astype(BF).astype(F32)
+    rest = value - first
+    second = rest.astype(BF).astype(F32)
+    third = rest - second
+    out = jnp.where(lane == 0, first, jnp.where(lane == 1, second, jnp.where(lane == 2, third, 0.0)))
+    return out.astype(BF)
+
+
+def first_keys(lengths_ref, at):
+    count = lengths_ref.shape[1]
+    start = jnp.zeros_like(at)
+    begin = 0
+    for s in range(count):
+        start = jnp.where(at >= begin, begin, start)
+        begin = begin + lengths_ref[0, s]
+    padding = at >= begin
+    return jnp.where(padding, at, start), padding
+
+
+def front(cfg, lengths_ref, x_ref, do_ref, wq_ref, wk_ref, wv_ref, wo_ref, wg_ref, wu_ref, wd_ref, gpack_ref,
+          table_ref, begin_ref,
+          qx_out, kx_out, vx_out, dax_out, mo_out, pre_out, cs_out, xn_out, w_out, gwo_out, gwd_out, ggu_out,
+          hmid_out, dhmid_out, gains_out, gpost_out,
+          wsend, gsend, w, wo_all, gu_in, gu, wd_all, gpart, gbuf, gz, xg, xn, dob, pre, cs, qx, kx, vx, acc, attn,
+          dblk, act, dgu, mo, sib_out, sib_in, out, inn, keep, hres, hmid, dhmid, dax, gwo, gwd_buf, gwd_in, ggu_buf,
+          ggu_in, gwd, ggu, gpost, local, send, recv):
+    n, nz, ql, kvl, hd, ff = cfg["n"], cfg["nz"], cfg["ql"], cfg["kvl"], cfg["hd"], cfg["ff"]
     t, dm = x_ref.shape
+    half = t // 2
+    tiles = qx.shape[0]
+    rows = n * t
     net = Net(n, nz, send, recv)
     c, z = net.c, net.z
+    evens, odds = list(range(2, n, 2)), list(range(3, n, 2))
+    stores = []
+
+    def store(src, dst):
+        cp = pltpu.make_async_copy(src, dst, local.at[len(stores)])
+        cp.start()
+        stores.append(cp)
+        return cp
+
+    qw, kw = ql * hd, kvl * hd
+    for j in range(n):
+        wsend[j, :, :qw] = wq_ref[:, j * qw : (j + 1) * qw]
+        wsend[j, :, qw : qw + kw] = wk_ref[:, j * kw : (j + 1) * kw]
+        wsend[j, :, qw + kw :] = wv_ref[:, j * kw : (j + 1) * kw]
+        gsend[j, :, :ff] = wg_ref[:, j * ff : (j + 1) * ff]
+        gsend[j, :, ff:] = wu_ref[:, j * ff : (j + 1) * ff]
+    place = c * nz + z
+    share = dm // (n * nz)
+    at = lax.broadcasted_iota(jnp.int32, (8, LANES), 0) * LANES + lax.broadcasted_iota(jnp.int32, (8, LANES), 1)
+    here = (at >= place * share) & (at < (place + 1) * share)
+    gpart[0:8, :] = jnp.where(here, gpack_ref[0:1, :], 0.0)
+    gpart[8:16, :] = jnp.where(here, gpack_ref[1:2, :], 0.0)
+    share = hd // (n * nz)
+    here = (at >= place * share) & (at < (place + 1) * share)
+    gpart[16:24, :] = jnp.where(here, gpack_ref[2:3, :], 0.0) + jnp.where(
+        (at >= LANES + place * share) & (at < LANES + (place + 1) * share), gpack_ref[3:4, :], 0.0
+    )
     net.barrier()
     slot = 0
     plane = []
     for mask in range(1, n):
-        cp = net.copy(gains_ref, gbuf.at[c], slot + mask, net.peer(mask))
+        cp = net.copy(gpart, gbuf.at[c], slot + mask, net.peer(mask))
         cp.start()
         plane.append(cp)
     slot += n
     for mask in range(1, n):
-        cp = net.copy(wqkv_ref.at[net.at(mask)], w_ref.at[c, z], slot + mask, net.peer(mask))
+        cp = net.copy(wsend.at[net.at(mask)], w.at[c, z], slot + mask, net.peer(mask))
         cp.start()
         plane.append(cp)
     slot += n
-    line = []
+    line_wo = []
     for mask in range(1, nz):
-        cp = net.copy(wo_ref, wo_out.at[z], slot + mask, net.zpeer(mask))
-        cp.start()
-        line.append(cp)
+        cp = net.copy(wo_ref, wo_all.at[z], slot + mask, net.zpeer(mask))
+        cp.start()
+        line_wo.append(cp)
     slot += nz
     gath = Gather(net, x_ref, xg, slot)
     slot += n
     late = []
     for mask in range(1, n):
-        cp = net.copy(gu_ref.at[net.at(mask)], gu_out.at[c], slot + mask, net.peer(mask))
+        cp = net.copy(gsend.at[net.at(mask)], gu.at[c, z], slot + mask, net.peer(mask))
         cp.start()
         late.append(cp)
     slot += n
-    gbuf[c] = gains_ref[...]
-    w_ref[c, z] = wqkv_ref[c]
-    gu_out[c] = gu_ref[c]
-    wo_out[z] = wo_ref[...]
+    gbuf[c] = gpart[...]
+    w[c, z] = wsend[c]
+    gu[c, z] = gsend[c]
+    wo_all[z] = wo_ref[...]
+    wd_all[z] = wd_ref[...]
     xg[c] = x_ref[...]
     for cp in plane[: n - 1]:
         cp.wait_recv()
@@ -211,208 +267,213 @@
     slot += nz
     for cp in plane[n - 1 :]:
         cp.wait_recv()
+    line_w = []
     for mask in range(1, nz):
-        cp = net.copy(w_ref.at[:, z], w_ref.at[:, z], slot + mask, net.zpeer(mask))
-        cp.start()
-        line.append(cp)
+        cp = net.copy(w.at[:, z], w.at[:, z], slot + mask, net.zpeer(mask))
+        cp.start()
+        line_w.append(cp)
     slot += nz
+
+    lane = lax.broadcasted_iota(jnp.int32, (t, hd), 1)
+    for d in range(n):
+        u = lax.broadcasted_iota(jnp.int32, (t, hd), 0)
+        packed = jnp.where(u < half, d * half + u, (2 * n - 1 - d) * half + u - half)
+        mine = jnp.concatenate(
+            [table_ref[d * half : (d + 1) * half], table_ref[(2 * n - 1 - d) * half : (2 * n - d) * half]], axis=0
+        )
+        first = jnp.broadcast_to(begin_ref[0:1, :], (t, hd))
+        begin = 0
+        for s in range(lengths_ref.shape[1]):
+            if s:
+                first = jnp.where(packed >= begin, begin_ref[s : s + 1, :], first)
+            begin = begin + lengths_ref[0, s]
+        first = jnp.where(packed >= begin, mine, first)
+        mine_other, first_other = pltpu.roll(mine, hd // 2, 1), pltpu.roll(first, hd // 2, 1)
+        cs[d] = jnp.where(
+            lane < hd // 2, mine * first + mine_other * first_other, mine * first_other - mine_other * first
+        )
+
     for cp in gains_line:
         cp.wait_recv()
     gains = jnp.sum(gz[...], axis=0)
-    gains_out[...] = gains
     g_in = row_of(gains, 0, dm // LANES)
+    g_post = row_of(gains, 8, dm // LANES)
     g_q = gains[16:17, :]
     g_k = gains[17:18, :]
     step = 32
 
     def normalise(d):
-        def rows(i, carry):
-            at = pl.ds(pl.multiple_of(i * step, step), step)
-            x = xg[d, at, :].astype(F32)
-            r = lax.rsqrt(jnp.mean(x * x, axis=-1, keepdims=True) + cfg["eps"])
-            xn_ref[d, at, :] = (x * r * g_in).astype(BF)
+        def some(i, carry):
+            here = pl.ds(pl.multiple_of(i * step, step), step)
+            v = xg[d, here, :].astype(F32)
+            r = lax.rsqrt(jnp.mean(v * v, axis=-1, keepdims=True) + cfg["eps"])
+            xn[d, here, :] = (v * r * g_in).astype(BF)
             return carry
 
-        lax.fori_loop(0, t // step, rows, 0)
-
-    order = [0, 1] + [m for e in range(2, n, 2) for m in (e,)] + [m for e in range(2, n, 2) for m in (e + 1,)]
-    for mask in order:
+        lax.fori_loop(0, t // step, some, 0)
+
+    for mask in [0, 1] + evens:
         if mask:
             gath.arrive(mask)
         normalise(net.at(mask))
-    for cp in line:
+    for cp in late:
         cp.wait_recv()
-    w = w_ref[...].reshape(dm, -1)
+    line_gu = []
+    for mask in range(1, nz):
+        cp = net.copy(gu.at[:, z], gu.at[:, z], slot + mask, net.zpeer(mask))
+        cp.start()
+        line_gu.append(cp)
+    slot += nz
+    for mask in range(1, nz):
+        cp = net.copy(wd_ref, wd_all.at[z], slot + mask, net.zpeer(mask))
+        cp.start()
+        line_gu.append(cp)
+    slot += nz
+    u = lax.broadcasted_iota(jnp.int32, (t, 1), 0)
+    packed = jnp.where(u < half, c * half + u, (2 * n - 1 - c) * half + u - half)
+    padding = first_keys(lengths_ref, packed)[1]
+    dob[...] = jnp.where(padding, 0.0, do_ref[...].astype(F32)).astype(BF)
+    dblk[c] = dob[...]
+    gath_d = Gather(net, dob, dblk, slot)
+    slot += n
+    for mask in odds:
+        gath.arrive(mask)
+        normalise(net.at(mask))
+    for cp in line_w:
+        cp.wait_recv()
+    wqkv = w[...].reshape(dm, -1)
+    lane_b = lax.broadcasted_iota(jnp.int32, (half, hd), 1)
+    minus = jnp.where(lane_b < 3, -1.0, 0.0).astype(BF)
 
     def head_block(d, carry):
-        qkv = dot(xn_ref[d], w)
+        qkv = dot(xn[d], wqkv)
         width = (ql + kvl) * hd
-        pre_ref[d] = qkv[:, :width]
-        cos, sin = cos_ref[d], sin_ref[d]
-        places = half_places(net, d, t // 2)
+        pre[d] = qkv[:, :width]
+        both = cs[d]
+        other = pltpu.roll(both, hd // 2, 1)
+        cos = jnp.where(lane < hd // 2, both, other)
+        sin = jnp.where(lane < hd // 2, -other, both)
+        places = half_places(net, d, half)
         for h in range(ql + kvl):
             v = qkv[:, h * hd : (h + 1) * hd]
             r = lax.rsqrt(jnp.mean(v * v, axis=-1, keepdims=True) + cfg["eps"])
             hat = v * r * (g_q if h < ql else g_k)
             low = (hat * cos + pltpu.roll(hat, hd // 2, 1) * sin).astype(BF)
             for s, (tile, row) in enumerate(places):
-                part = low[s * (t // 2) : (s + 1) * (t // 2)]
+                part = low[s * half : (s + 1) * half]
                 if h < ql:
-                    q_ref[tile, h, pl.ds(row, t // 2), :] = part
+                    qx[tile, h, pl.ds(row, half), :hd] = part
                 else:
-                    k_ref[tile, h - ql, pl.ds(row, t // 2), :] = part
-        for h in range(kvl):
-            low = qkv[:, width + h * hd : width + (h + 1) * hd].astype(BF)
-            for s, (tile, row) in enumerate(places):
-                v_ref[tile, h, pl.ds(row, t // 2), :] = low[s * (t // 2) : (s + 1) * (t // 2)]
+                    kx[tile, pl.ds(row, half), :hd] = part
+        low = qkv[:, width:].astype(BF)
+        for s, (tile, row) in enumerate(places):
+            vx[tile, pl.ds(row, half), :hd] = low[s * half : (s + 1) * half]
+            kx[tile, pl.ds(row, half), hd:] = minus
+            vx[tile, pl.ds(row, half), hd:] = minus
         return carry
 
     lax.fori_loop(0, n, head_block, 0)
-    for cp in late:
-        cp.wait_recv()
-    gath.finish()
-    for cp in plane + line + gains_line + late:
-        cp.wait_send()
-
-
-def attend(cfg, q_ref, k_ref, v_ref, start_ref, db_ref, gu_ref,
-           attn_ref, qx_ref, dblk_ref, gu_out,
-           vx, acc, send, recv):
-    n, nz, ql, hd = cfg["n"], cfg["nz"], cfg["ql"], cfg["hd"]
-    tiles = q_ref.shape[0]
-    net = Net(n, nz, send, recv)
-    c, z = net.c, net.z
-    net.barrier()
-    line = []
-    for mask in range(1, nz):
-        cp = net.copy(gu_ref, gu_out.at[:, z], mask, net.zpeer(mask))
-        cp.start()
-        line.append(cp)
-    gath = Gather(net, db_ref, dblk_ref, nz)
-    gu_out[:, z] = gu_ref[...]
-    dblk_ref[c] = db_ref[...]
-    rows = ql * TILE
+    xn_stored = store(xn, xn_out)
+    store(pre, pre_out)
+    store(cs, cs_out)
+    store(kx, kx_out)
+    store(vx, vx_out)
+    store(w, w_out)
+
+    wide = ql * TILE
     factor = math.log2(math.e) / math.sqrt(hd)
-    vx[:, :, :hd] = v_ref[:, 0]
-    vx[:, :, hd:] = jnp.ones((tiles, TILE, hd), BF)
-    lane = lax.broadcasted_iota(jnp.int32, (rows, hd), 1)
+    lane_q = lax.broadcasted_iota(jnp.int32, (wide, hd), 1)
 
     def q_tile(i, carry):
-        q = q_ref[i].reshape(rows, hd)
-        start = start_ref[pl.ds(pl.multiple_of(i * TILE, TILE), TILE), :]
+        q = qx[i, :, :, :hd].reshape(wide, hd)
+        start = first_keys(lengths_ref, i * TILE + lax.broadcasted_iota(jnp.int32, (TILE, 1), 0))[0]
         q_at = i * TILE + lax.broadcasted_iota(jnp.int32, (TILE, TILE), 0)
         acc[...] = jnp.zeros_like(acc)
 
         def k_tile(j, carry):
-            s = dot_rt(q, k_ref[j, 0])
+            s = dot_rt(q, kx[j, :, :hd])
             k_at = j * TILE + lax.broadcasted_iota(jnp.int32, (TILE, TILE), 1)
             allowed = (k_at <= q_at) & (k_at >= start)
             e = jnp.where(allowed[None], jnp.exp2(s * factor).reshape(ql, TILE, TILE), 0.0)
-            acc[...] += dot(e.astype(BF).reshape(rows, TILE), vx[j])
+            acc[...] += dot(e.astype(BF).reshape(wide, TILE), vx[j])
             return carry
 
         lax.fori_loop(jnp.maximum(i - cfg["window"], 0), i + 1, k_tile, 0)
-        total = acc[:, hd:]
-        attn = acc[:, :hd] / total
+        total = -acc[:, hd : hd + 1]
+        low = (acc[:, :hd] / total).astype(BF)
         for h in range(ql):
-            attn_ref[pl.ds(pl.multiple_of(i * TILE, TILE), TILE), h * hd : (h + 1) * hd] = attn[
-                h * TILE : (h + 1) * TILE
-            ].astype(BF)
-        extra = jnp.log(total) * math.sqrt(hd)
-        qx_ref[i, :, :, :hd] = q_ref[i]
-        qx_ref[i, :, :, hd:] = split_three(extra, lane).reshape(ql, TILE, hd)
+            attn[pl.ds(pl.multiple_of(i * TILE, TILE), TILE), h * hd : (h + 1) * hd] = low[h * TILE : (h + 1) * TILE]
+        extra = jnp.broadcast_to(jnp.log(total) * math.sqrt(hd), (wide, hd))
+        qx[i, :, :, hd:] = split_three(extra, lane_q).reshape(ql, TILE, hd)
         return carry
 
-    lax.fori_loop(0, tiles, q_tile, 0)
-    for mask in list(range(2, n, 2)) + [1] + list(range(3, n, 2)):
-        gath.arrive(mask)
-    for cp in line:
+    lax.fori_loop(0, tiles // 2, q_tile, 0)
+    for mask in evens:
+        gath_d.arrive(mask)
+    lax.fori_loop(tiles // 2, tiles, q_tile, 0)
+    store(qx, qx_out)
+    for cp in line_wo:
         cp.wait_recv()
-    gath.finish()
-    for cp in line:
-        cp.wait_send()
-
-
-def split_three(value, lane):
-    first = value.astype(BF).astype(F32)
-    rest = value - first
-    second = rest.astype(BF).astype(F32)
-    third = rest - second
-    out = jnp.where(lane == 0, first, jnp.where(lane == 1, second, jnp.where(lane == 2, third, 0.0)))
-    return out.astype(BF)
-
-
-def feed(cfg, attn_ref, x_ref, dblk_ref, wo_ref, gu_ref, wd_ref, gains_ref,
-         mo_ref, dax_ref, hmid_ref, dhmid_ref, gwo_ref, gwd_ref, ggu_ref, gpost_ref,
-         wd_all, hn, act, dgu, dres, gwd_buf, ggu_buf, gwd_in, ggu_in, *rest):
-    n, nz, ql, hd, ff = cfg["n"], cfg["nz"], cfg["ql"], cfg["hd"], cfg["ff"]
-    first, second, (hres, send, recv) = rest[:5], rest[5:10], rest[10:]
-    t, dm = x_ref.shape
-    half = t // 2
-    net = Net(n, nz, send, recv)
-    c, z = net.c, net.z
-    net.barrier()
-    slot = 0
-    line = []
-    for mask in range(1, nz):
-        cp = net.copy(wd_ref, wd_all.at[z], slot + mask, net.zpeer(mask))
-        cp.start()
-        line.append(cp)
-    slot += nz
-    wd_all[z] = wd_ref[...]
-    wo = wo_ref[...].reshape(-1, dm)
+    wout = wo_all[...].reshape(-1, dm)
 
     def attn_rows(d):
         return jnp.concatenate(
-            [attn_ref[pl.ds(pl.multiple_of(b * half, half), half), :] for b in (d, 2 * n - 1 - d)], axis=0
+            [attn[pl.ds(pl.multiple_of(b * half, half), half), :] for b in (d, 2 * n - 1 - d)], axis=0
         )
 
-    sum1 = PlaneSum(net, *first, slot)
-    slot += n
-    for mask in list(range(2, n, 2))[::-1] + [0]:
-        sum1.give_sibling(mask, dot(attn_rows(net.at(mask + 1)), wo))
-        sum1.give(mask, dot(attn_rows(net.at(mask)), wo))
-    g_post = row_of(gains_ref[...], 8, dm // LANES)
+    xn_stored.wait()
+    hn, dres = xn, xg
+    gath.finish()
+    sum1 = PlaneSum(net, sib_out, sib_in, out, inn, keep, slot)
+    slot += n
+    for mask in evens[::-1] + [0]:
+        sum1.give_sibling(mask, dot(attn_rows(net.at(mask + 1)), wout))
+        sum1.give(mask, dot(attn_rows(net.at(mask)), wout))
+    for mask in [1] + odds:
+        gath_d.arrive(mask)
+    for cp in line_gu:
+        cp.wait_recv()
     h_mid = x_ref[...].astype(F32) + sum1.total()
-    hmid_ref[...] = h_mid
+    hmid[...] = h_mid
     r_mid = lax.rsqrt(jnp.mean(h_mid * h_mid, axis=-1, keepdims=True) + cfg["eps"])
     hres[...] = (h_mid * r_mid * g_post).astype(BF)
     gath1 = Gather(net, hres, hn, slot)
     slot += n
     hn[c] = hres[...]
-    for cp in line:
-        cp.wait_recv()
-    wgu = gu_ref[...].reshape(dm, -1)
+    store(hmid, hmid_out)
+    sum1.finish()
+    wgu = gu[...].reshape(dm, -1)
     wd = wd_all[...].reshape(-1, dm)
 
+    mo_stores = []
+
     def block(d):
-        gu = dot(hn[d], wgu)
-        gate, up = gu[:, :ff], gu[:, ff:]
+        both = dot(hn[d], wgu)
+        gate, up = both[:, :ff], both[:, ff:]
         sig = 1.0 / (1.0 + jnp.exp(-gate))
         silu = gate * sig
         low = (silu * up).astype(BF)
         act[d] = low
-        mo_ref[d] = dot(low, wd).astype(BF)
-        d_act = dot_rt(dblk_ref[d], wd)
-        d_gate = (d_act * up * sig * (1.0 + gate * (1.0 - sig))).astype(BF)
-        d_up = (d_act * silu).astype(BF)
-        dgu[d, :, :ff] = d_gate
-        dgu[d, :, ff:] = d_up
+        if len(mo_stores) > 1:
+            mo_stores[-2].wait()
+        place = len(mo_stores) % 2
+        mo[place] = dot(low, wd).astype(BF)
+        mo_stores.append(store(mo.at[place], mo_out.at[d]))
+        d_act = dot_rt(dblk[d], wd)
+        dgu[d, :, :ff] = (d_act * up * sig * (1.0 + gate * (1.0 - sig))).astype(BF)
+        dgu[d, :, ff:] = (d_act * silu).astype(BF)
         return dot_rt(dgu[d], wgu)
 
-    sum2 = PlaneSum(net, *second, slot)
+    sum2 = PlaneSum(net, sib_out, sib_in, out, inn, keep, slot)
     slot += n
     for mask in range(0, n, 2):
         if mask:
             gath1.arrive(mask)
-            gath1.arrive(mask + 1)
-        else:
-            gath1.arrive(1)
+        gath1.arrive(mask + 1)
         sum2.give_sibling(mask, block(net.at(mask + 1)))
         sum2.give(mask, block(net.at(mask)))
-    rows = n * t
     dgu_all = dgu[...].reshape(rows, 2 * ff)
-    gwd_buf[...] = dot_lt(act[...].reshape(rows, ff), dblk_ref[...].reshape(rows, dm)).astype(BF).reshape(gwd_buf.shape)
+    gwd_buf[...] = dot_lt(act[...].reshape(rows, ff), dblk[...].reshape(rows, dm)).astype(BF).reshape(gwd_buf.shape)
     gline = []
     for mask in range(1, nz):
         cp = net.copy(gwd_buf.at[net.zat(mask)], gwd_in.at[mask - 1], slot + mask, net.zpeer(mask))
@@ -421,9 +482,9 @@
     slot += nz
     per = dm // n
     cols = 2
-    wide = dm // cols
+    part_w = dm // cols
     for j in range(cols):
-        part = dot_lt(hn[:, :, j * wide : (j + 1) * wide].reshape(rows, wide), dgu_all)
+        part = dot_lt(hn[:, :, j * part_w : (j + 1) * part_w].reshape(rows, part_w), dgu_all)
         ggu_buf[j * (n // cols) : (j + 1) * (n // cols)] = part.astype(BF).reshape(n // cols, nz, per // nz, 2 * ff)
     for mask in range(1, nz):
         cp = net.copy(ggu_buf.at[:, net.zat(mask)], ggu_in.at[mask - 1], slot + mask, net.zpeer(mask))
@@ -431,96 +492,110 @@
         gline.append(cp)
     slot += nz
     d_hn = sum2.total()
-    v = hmid_ref[...]
+    v = hmid[...]
     r = lax.rsqrt(jnp.mean(v * v, axis=-1, keepdims=True) + cfg["eps"])
-    gpost_ref[...] = jnp.sum(d_hn * v * r, axis=0, keepdims=True)
+    gpost[...] = jnp.sum(d_hn * v * r, axis=0, keepdims=True)
     gdy = g_post * d_hn
-    d_hmid = dblk_ref[c].astype(F32) + r * gdy - v * (r * r * r) * jnp.mean(gdy * v, axis=-1, keepdims=True)
-    dhmid_ref[...] = d_hmid
+    d_hmid = dblk[c].astype(F32) + r * gdy - v * (r * r * r) * jnp.mean(gdy * v, axis=-1, keepdims=True)
+    dhmid[...] = d_hmid
     gath1.finish()
     hres[...] = d_hmid.astype(BF)
     gath2 = Gather(net, hres, dres, slot)
     slot += n
     dres[c] = hres[...]
-    lane = lax.broadcasted_iota(jnp.int32, (half, hd), 1)
+    store(dhmid, dhmid_out)
 
     def back(d):
-        d_attn = dot_rt(dres[d], wo)
+        d_attn = dot_rt(dres[d], wout)
         for s, (tile, row) in enumerate(half_places(net, d, half)):
             b = (d, 2 * n - 1 - d)[s]
-            attn = attn_ref[pl.ds(pl.multiple_of(b * half, half), half), :].astype(F32)
+            rows_b = attn[pl.ds(pl.multiple_of(b * half, half), half), :].astype(F32)
             low = d_attn[s * half : (s + 1) * half].astype(BF)
-            prod = low.astype(F32) * attn
+            prod = low.astype(F32) * rows_b
             for h in range(ql):
                 delta = jnp.sum(prod[:, h * hd : (h + 1) * hd], axis=-1, keepdims=True)
-                dax_ref[tile, h, pl.ds(row, half), :hd] = low[:, h * hd : (h + 1) * hd]
-                dax_ref[tile, h, pl.ds(row, half), hd:] = split_three(jnp.broadcast_to(delta, (half, hd)), lane)
+                dax[tile, h, pl.ds(row, half), :hd] = low[:, h * hd : (h + 1) * hd]
+                dax[tile, h, pl.ds(row, half), hd:] = split_three(jnp.broadcast_to(delta, (half, hd)), lane_b)
 
     back(c)
-    for mask in [1] + list(range(2, n, 2)) + list(range(3, n, 2)):
+    for mask in [1] + evens + odds:
         gath2.arrive(mask)
         back(net.at(mask))
+    store(dax, dax_out)
     total = None
     for s in range(2):
-        blocks = attn_ref[s * (rows // 2) : (s + 1) * (rows // 2), :]
+        blocks = attn[s * (rows // 2) : (s + 1) * (rows // 2), :]
         if s:
             blocks = jnp.concatenate([blocks[(n - 1 - i) * half : (n - i) * half] for i in range(n)], axis=0)
         part = dot_lt(blocks, dres[:, s * half : (s + 1) * half, :].reshape(n * half, dm))
         total = part if total is None else total + part
-    gwo_ref[...] = total.astype(BF).reshape(gwo_ref.shape)
+    gwo[...] = total.astype(BF).reshape(gwo.shape)
+    store(gwo, gwo_out)
     for cp in gline:
         cp.wait_recv()
-    gwd = gwd_buf[z].astype(F32)
-    ggu = ggu_buf[:, z].astype(F32)
+    gwd_sum = gwd_buf[z].astype(F32)
+    ggu_sum = ggu_buf[:, z].astype(F32)
     for i in range(nz - 1):
-        gwd = gwd + gwd_in[i].astype(F32)
-        ggu = ggu + ggu_in[i].astype(F32)
-    gwd_ref[...] = gwd
-    ggu_ref[...] = ggu.astype(BF)
-    for part in (sum1, sum2, gath2):
+        gwd_sum = gwd_sum + gwd_in[i].astype(F32)
+        ggu_sum = ggu_sum + ggu_in[i].astype(F32)
+    gwd[...] = gwd_sum
+    ggu[...] = ggu_sum.astype(BF)
+    store(gwd, gwd_out)
+    store(ggu, ggu_out)
+    gains_out[...] = gains
+    gpost_out[...] = gpost[...]
+    for part in (gath_d, sum2, gath2):
         part.finish()
-    for cp in line + gline:
+    for cp in plane + line_wo + late + gains_line + line_w + line_gu + gline:
         cp.wait_send()
-
-
-def attend_back(cfg, qx_ref, k_ref, v_ref, dax_ref, start_ref, mo_ref, hmid_ref, valid_ref, gwo_ref, ggu_ref,
-                dq_ref, dk_ref, dv_ref, block_ref, gwo_out, ggate_ref, gup_ref,
-                kx, vx, dk_acc, dv_acc, gwo_in, ggu_in, *rest):
-    n, nz, ql, hd, ff = cfg["n"], cfg["nz"], cfg["ql"], cfg["hd"], cfg["ff"]
-    sums, (send, recv) = rest[:5], rest[5:]
+    for cp in stores:
+        if not any(cp is other for other in [xn_stored] + mo_stores[:-2]):
+            cp.wait()
+
+
+def back(cfg, lengths_ref, qx_ref, kx_ref, vx_ref, dax_ref, mo_ref, pre_ref, cs_ref, xn_ref, w_ref, gwo_ref, ggu_ref,
+         hmid_ref, dhmid_ref, gains_ref, gpost_ref, x_ref,
+         block_out, dx_out, gwo_out, ggu_out, gqkv_out, gains_out,
+         mo_own, mo_in, mo_send, mo_recv, pre, cs, xn, w, hmid, dhmid, dq, dk, dv, dk_acc, dv_acc, gwo_in,
+         ggu_in, dqkv, gbuf, g_line, gsum, g_in, part, gplane, gz, sib_out, sib_in, out, inn, keep, local, send, recv):
+    n, nz, ql, kvl, hd, ff = cfg["n"], cfg["nz"], cfg["ql"], cfg["kvl"], cfg["hd"], cfg["ff"]
+    t, dm = x_ref.shape
+    half = t // 2
+    rows = n * t
     tiles = qx_ref.shape[0]
     net = Net(n, nz, send, recv)
     c, z = net.c, net.z
+    evens = list(range(2, n, 2))
+    loads = []
+
+    def load(src, dst):
+        cp = pltpu.make_async_copy(src, dst, local.at[len(loads)])
+        cp.start()
+        loads.append(cp)
+        return cp
+
+    own = [load(mo_ref.at[net.at(mask)], mo_own.at[mask // 2]) for mask in range(0, n, 2)]
     net.barrier()
     slot = 0
-    sum1 = PlaneSum(net, *sums, slot)
-    slot += n
-    for mask in list(range(2, n, 2))[::-1] + [0]:
-        sum1.give_sibling(mask, mo_ref[net.at(mask + 1)])
-    for mask in list(range(2, n, 2))[::-1] + [0]:
-        sum1.give(mask, mo_ref[net.at(mask)].astype(F32))
+    plane = []
+    for mask in evens[::-1] + [0]:
+        cp = net.copy(mo_ref.at[net.at(mask + 1)], mo_in.at[mask // 2], slot + mask + 1, net.peer(1))
+        cp.start()
+        plane.append(cp)
+    first_sums = dict(zip(evens[::-1] + [0], plane))
     line = []
+    sum_slot = slot
+    slot += n
     for mask in range(1, nz):
         cp = net.copy(gwo_ref.at[net.zat(mask)], gwo_in.at[mask - 1], slot + mask, net.zpeer(mask))
         cp.start()
         line.append(cp)
     slot += nz
-    for mask in range(1, n):
-        cp = net.copy(ggu_ref.at[net.at(mask)], ggu_in.at[c], slot + mask, net.peer(mask))
-        cp.start()
-        line.append(cp)
-    slot += n
-    ggu_in[c] = ggu_ref[c]
-    rows = ql * TILE
+    more = [load(a, b) for a, b in ((pre_ref, pre), (cs_ref, cs), (xn_ref, xn), (w_ref, w), (hmid_ref, hmid), (dhmid_ref, dhmid))]
+    wide = ql * TILE
     factor = math.log2(math.e) / math.sqrt(hd)
     scale = 1.0 / math.sqrt(hd)
-    lane = lax.broadcasted_iota(jnp.int32, (tiles, TILE, hd), 2)
-    minus = jnp.where(lane < 3, -1.0, 0.0).astype(BF)
-    kx[:, :, :hd] = k_ref[:, 0]
-    kx[:, :, hd:] = minus
-    vx[:, :, :hd] = v_ref[:, 0]
-    vx[:, :, hd:] = minus
-    dq_ref[...] = jnp.zeros_like(dq_ref)
+    dq[...] = jnp.zeros_like(dq)
 
     def k_tile(j, carry):
         k_at = j * TILE + lax.broadcasted_iota(jnp.int32, (TILE, TILE), 0)
@@ -528,123 +603,121 @@
         dv_acc[...] = jnp.zeros_like(dv_acc)
 
         def q_tile(i, carry):
-            qx = qx_ref[i].reshape(rows, 2 * hd)
-            dax = dax_ref[i].reshape(rows, 2 * hd)
-            start = start_ref[:, pl.ds(pl.multiple_of(i * TILE, TILE), TILE)]
+            qx = qx_ref[i].reshape(wide, 2 * hd)
+            dax = dax_ref[i].reshape(wide, 2 * hd)
+            start = first_keys(lengths_ref, i * TILE + lax.broadcasted_iota(jnp.int32, (1, TILE), 1))[0]
             q_at = i * TILE + lax.broadcasted_iota(jnp.int32, (TILE, TILE), 1)
             allowed = (k_at <= q_at) & (k_at >= start)
             allowed = jnp.concatenate([allowed] * ql, axis=1)
-            s = dot_rt(kx[j], qx)
+            s = dot_rt(kx_ref[j], qx)
             p = jnp.where(allowed, jnp.exp2(s * factor), 0.0)
-            ds = (p * dot_rt(vx[j], dax)).astype(BF)
+            ds = (p * dot_rt(vx_ref[j], dax)).astype(BF)
             dv_acc[...] += dot(p.astype(BF), dax[:, :hd])
             dk_acc[...] += dot(ds, qx[:, :hd])
-            dq_ref[i] += dot_lt(ds, k_ref[j, 0])
+            dq[i] += dot_lt(ds, kx_ref[j, :, :hd])
             return carry
 
         lax.fori_loop(j, jnp.minimum(j + cfg["window"], tiles - 1) + 1, q_tile, 0)
-        dk_ref[j] = dk_acc[...] * scale
-        dv_ref[j] = dv_acc[...]
+        dk[j] = dk_acc[...] * scale
+        dv[j] = dv_acc[...]
         return carry
 
-    lax.fori_loop(0, tiles, k_tile, 0)
-    dq_ref[...] = dq_ref[...] * scale
-    for cp in line:
-        cp.wait_recv()
-    gwo = gwo_ref[z].astype(F32)
-    for i in range(nz - 1):
-        gwo = gwo + gwo_in[i].astype(F32)
-    gwo_out[...] = gwo
-    for d in range(n):
-        both = ggu_in[d].astype(F32)
-        ggate_ref[:, d * ff : (d + 1) * ff] = both[:, :ff]
-        gup_ref[:, d * ff : (d + 1) * ff] = both[:, ff:]
-    block_ref[...] = (valid_ref[...] * (hmid_ref[...] + sum1.total())).astype(BF)
-    sum1.finish()
-    for cp in line:
-        cp.wait_send()
-
-
-def head_back(cfg, pre_ref, dq_ref, dk_ref, dv_ref, cos_ref, sin_ref, gains_ref, xn_ref, w_ref, x_ref, dhmid_ref,
-              gpost_ref,
-              dx_ref, gq_ref, gk_ref, gv_ref, gains_out,
-              dqkv, gbuf, g_in_line, gsum, g_in, part, gplane, gz, *rest):
-    n, nz, ql, kvl, hd = cfg["n"], cfg["nz"], cfg["ql"], cfg["kvl"], cfg["hd"]
-    sums, (send, recv) = rest[:5], rest[5:]
-    t, dm = x_ref.shape
-    half = t // 2
-    net = Net(n, nz, send, recv)
-    c, z = net.c, net.z
-    net.barrier()
+    lax.fori_loop(0, tiles // 4, k_tile, 0)
+    second = {}
+    for mask in evens[::-1]:
+        i = mask // 2
+        own[i].wait()
+        first_sums[mask].wait_recv()
+        mo_send[i - 1] = (mo_own[i].astype(F32) + mo_in[i].astype(F32)).astype(BF)
+        cp = net.copy(mo_send.at[i - 1], mo_recv.at[i - 1], sum_slot + mask, net.peer(mask))
+        cp.start()
+        plane.append(cp)
+        second[mask] = cp
+    for mask in range(1, n):
+        cp = net.copy(ggu_ref.at[net.at(mask)], ggu_in.at[c], slot + mask, net.peer(mask))
+        cp.start()
+        line.append(cp)
+    slot += n
+    ggu_in[c] = ggu_ref[c]
+    lax.fori_loop(tiles // 4, tiles, k_tile, 0)
+    for cp in more:
+        cp.wait()
     gains = gains_ref[...]
-    w = w_ref[...].reshape(dm, -1)
+    lane = lax.broadcasted_iota(jnp.int32, (t, hd), 1)
 
     def head_block(d, carry):
-        pre = pre_ref[d]
-        cos, sin = cos_ref[d], sin_ref[d]
+        before = pre[d]
+        both = cs[d]
+        other = pltpu.roll(both, hd // 2, 1)
+        cos = jnp.where(lane < hd // 2, both, other)
+        sin = jnp.where(lane < hd // 2, -other, both)
         places = half_places(net, d, half)
         new = []
         for h in range(ql + kvl):
             if h < ql:
-                dy = jnp.concatenate([dq_ref[tile, pl.ds(h * TILE + row, half), :] for tile, row in places], axis=0)
+                dy = jnp.concatenate([dq[tile, pl.ds(h * TILE + row, half), :] for tile, row in places], axis=0) * scale
             else:
-                dy = jnp.concatenate([dk_ref[tile, pl.ds(row, half), :] for tile, row in places], axis=0)
+                dy = jnp.concatenate([dk[tile, pl.ds(row, half), :] for tile, row in places], axis=0)
             g = gains[16:17, :] if h < ql else gains[17:18, :]
-            v = pre[:, h * hd : (h + 1) * hd]
+            v = before[:, h * hd : (h + 1) * hd]
             r = lax.rsqrt(jnp.mean(v * v, axis=-1, keepdims=True) + cfg["eps"])
             dy = dy * cos - pltpu.roll(dy, hd // 2, 1) * sin
             new.append(jnp.sum(dy * v * r, axis=0, keepdims=True))
             gdy = g * dy
-            dv = r * gdy - v * (r * r * r) * jnp.mean(gdy * v, axis=-1, keepdims=True)
-            dqkv[d, :, h * hd : (h + 1) * hd] = dv.astype(BF)
-        dv = jnp.concatenate([dv_ref[tile, pl.ds(row, half), :] for tile, row in places], axis=0)
-        dqkv[d, :, (ql + kvl) * hd :] = dv.astype(BF)
+            dpre = r * gdy - v * (r * r * r) * jnp.mean(gdy * v, axis=-1, keepdims=True)
+            dqkv[d, :, h * hd : (h + 1) * hd] = dpre.astype(BF)
+        dval = jnp.concatenate([dv[tile, pl.ds(row, half), :] for tile, row in places], axis=0)
+        dqkv[d, :, (ql + kvl) * hd :] = dval.astype(BF)
         q_sum = sum(new[1:ql], new[0])
         k_sum = sum(new[ql + 1 :], new[ql])
         return (carry[0] + q_sum, carry[1] + k_sum)
 
     zero = jnp.zeros((1, hd), F32)
     gq, gk = lax.fori_loop(0, n, head_block, (zero, zero))
-    rows = n * t
+    wqkv = w[...].reshape(dm, -1)
+    sum1 = PlaneSum(net, sib_out, sib_in, out, inn, keep, slot)
+    slot += n
+    for mask in evens[::-1] + [0]:
+        sum1.give_sibling(mask, dot_rt(dqkv[net.at(mask + 1)], wqkv))
+        sum1.give(mask, dot_rt(dqkv[net.at(mask)], wqkv))
     per = dm // n
     cols = 2
-    wide = dm // cols
+    part_w = dm // cols
     d_all = dqkv[...].reshape(rows, -1)
     for j in range(cols):
-        grad = dot_lt(xn_ref[:, :, j * wide : (j + 1) * wide].reshape(rows, wide), d_all)
+        grad = dot_lt(xn[:, :, j * part_w : (j + 1) * part_w].reshape(rows, part_w), d_all)
         gbuf[j * (n // cols) : (j + 1) * (n // cols)] = grad.astype(BF).reshape(n // cols, nz, per // nz, -1)
-    slot = 0
-    line = []
+    gline = []
     for mask in range(1, nz):
-        cp = net.copy(gbuf.at[:, net.zat(mask)], g_in_line.at[mask - 1], slot + mask, net.zpeer(mask))
-        cp.start()
-        line.append(cp)
+        cp = net.copy(gbuf.at[:, net.zat(mask)], g_line.at[mask - 1], slot + mask, net.zpeer(mask))
+        cp.start()
+        gline.append(cp)
     slot += nz
-    sum1 = PlaneSum(net, *sums, slot)
-    slot += n
-    for mask in list(range(2, n, 2))[::-1] + [0]:
-        sum1.give_sibling(mask, dot_rt(dqkv[net.at(mask + 1)], w))
-        sum1.give(mask, dot_rt(dqkv[net.at(mask)], w))
+    own[0].wait()
+    total = hmid[...] + mo_own[0].astype(F32)
+    first_sums[0].wait_recv()
+    total = total + mo_in[0].astype(F32)
+    for mask in evens:
+        second[mask].wait_recv()
+        total = total + mo_recv[mask // 2 - 1].astype(F32)
+    u = lax.broadcasted_iota(jnp.int32, (t, 1), 0)
+    packed = jnp.where(u < half, c * half + u, (2 * n - 1 - c) * half + u - half)
+    padding = first_keys(lengths_ref, packed)[1]
+    block_out[...] = jnp.where(padding, 0.0, total).astype(BF)
     for cp in line:
         cp.wait_recv()
-    total = gbuf[:, z].astype(F32)
+    gwo_sum = gwo_ref[z].astype(F32)
     for i in range(nz - 1):
-        total = total + g_in_line[i].astype(F32)
-    gsum[...] = total.astype(BF)
-    plane = []
-    for mask in range(1, n):
-        cp = net.copy(gsum.at[net.at(mask)], g_in.at[c], slot + mask, net.peer(mask))
-        cp.start()
-        plane.append(cp)
-    slot += n
-    g_in[c] = gsum[c]
+        gwo_sum = gwo_sum + gwo_in[i].astype(F32)
+    gwo_out[...] = gwo_sum
+    ggu_out[...] = ggu_in[...]
     d_xn = sum1.total()
     x = x_ref[...].astype(F32)
     g = row_of(gains, 0, dm // LANES)
     r = lax.rsqrt(jnp.mean(x * x, axis=-1, keepdims=True) + cfg["eps"])
     grad_in = jnp.sum(d_xn * x * r, axis=0, keepdims=True)
     gdy = g * d_xn
-    dx_ref[...] = dhmid_ref[...] + r * gdy - x * (r * r * r) * jnp.mean(gdy * x, axis=-1, keepdims=True)
+    dx_out[...] = dhmid[...] + r * gdy - x * (r * r * r) * jnp.mean(gdy * x, axis=-1, keepdims=True)
     part[...] = jnp.zeros_like(part)
     for j in range(dm // LANES):
         part[j : j + 1, :] = grad_in[:, j * LANES : (j + 1) * LANES]
@@ -658,57 +731,82 @@
         small.append(cp)
     slot += n
     gplane[c] = part[...]
+    for cp in gline:
+        cp.wait_recv()
+    qkv_sum = gbuf[:, z].astype(F32)
+    for i in range(nz - 1):
+        qkv_sum = qkv_sum + g_line[i].astype(F32)
+    gsum[...] = qkv_sum.astype(BF)
+    for mask in range(1, n):
+        cp = net.copy(gsum.at[net.at(mask)], g_in.at[c], slot + mask, net.peer(mask))
+        cp.start()
+        gline.append(cp)
+    slot += n
+    g_in[c] = gsum[c]
     for cp in small:
         cp.wait_recv()
     gz[z] = jnp.sum(gplane[...], axis=0)
-    last = []
     for mask in range(1, nz):
         cp = net.copy(gz.at[z], gz.at[z], slot + mask, net.zpeer(mask))
         cp.start()
-        last.append(cp)
-    for cp in plane:
+        small.append(cp)
+    for cp in gline[nz - 1 :]:
         cp.wait_recv()
-    qw, kw = ql * hd, kvl * hd
-    for d in range(n):
-        both = g_in[d].astype(F32)
-        gq_ref[:, d * qw : (d + 1) * qw] = both[:, :qw]
-        gk_ref[:, d * kw : (d + 1) * kw] = both[:, qw : qw + kw]
-        gv_ref[:, d * kw : (d + 1) * kw] = both[:, qw + kw :]
-    for cp in last:
+    gqkv_out[...] = g_in[...]
+    for cp in small[n - 1 :]:
         cp.wait_recv()
     gains_out[...] = jnp.sum(gz[...], axis=0)
     sum1.finish()
-    for cp in line + plane + small + last:
+    for cp in line + plane + small + gline:
         cp.wait_send()
 
 
-def call(body, cfg, outs, scratch, cid, *args):
-    slots = cfg["slots"]
+def finish(cfg, block_ref, dx_ref, gwo_ref, gwd_ref, ggu_ref, gqkv_ref, gains_ref,
+           block_out, dx_out, gin_out, gq_out, gk_out, gv_out, gqg_out, gkg_out, gwo_out, gpost_out, ggate_out, gup_out,
+           gwd_out):
+    n, nz, ql, kvl, hd, ff = cfg["n"], cfg["nz"], cfg["ql"], cfg["kvl"], cfg["hd"], cfg["ff"]
+    block_out[...] = block_ref[...]
+    dx_out[...] = dx_ref[...]
+    gwo_out[...] = gwo_ref[...]
+    gwd_out[...] = gwd_ref[...]
+    qw, kw = ql * hd, kvl * hd
+    for d in range(n):
+        both = gqkv_ref[d].astype(F32)
+        gq_out[:, d * qw : (d + 1) * qw] = both[:, :qw]
+        gk_out[:, d * kw : (d + 1) * kw] = both[:, qw : qw + kw]
+        gv_out[:, d * kw : (d + 1) * kw] = both[:, qw + kw :]
+        both = ggu_ref[d].astype(F32)
+        ggate_out[:, d * ff : (d + 1) * ff] = both[:, :ff]
+        gup_out[:, d * ff : (d + 1) * ff] = both[:, ff:]
+    place = lax.axis_index("ctx") * nz + lax.axis_index("fsdp")
+    for first, ref in ((0, gin_out), (8, gpost_out), (16, gqg_out), (17, gkg_out)):
+        width = ref.shape[1]
+        at = place * width
+        row = gains_ref[pl.ds(first + lax.div(at, LANES), 1), :]
+        ref[...] = pltpu.roll(row, lax.rem(LANES - lax.rem(at, LANES), LANES), 1)[:, :width]
+
+
+def call(body, cfg, ins, outs, scratch, cid, *args):
+    remote = cid is not None
+    params = dict(collective_id=cid, has_side_effects=True) if remote else {}
+    if remote:
+        sems = pltpu.SemaphoreType.DMA((cfg["slots"],))
+        scratch = scratch + [pltpu.SemaphoreType.DMA((32,)), sems, sems]
     return pl.pallas_call(
         functools.partial(body, cfg),
-        out_shape=[jax.ShapeDtypeStruct(shape, dtype) for shape, dtype in outs],
-        in_specs=[VMEM] * len(args),
-        out_specs=[VMEM] * len(outs),
-        scratch_shapes=scratch + [pltpu.SemaphoreType.DMA((slots,)), pltpu.SemaphoreType.DMA((slots,))],
-        compiler_params=pltpu.CompilerParams(collective_id=cid, has_side_effects=True, vmem_limit_bytes=LIMIT),
+        out_shape=[jax.ShapeDtypeStruct(shape, dtype) for shape, dtype, *_ in outs],
+        in_specs=ins,
+        out_specs=[o[2] if len(o) > 2 else VMEM for o in outs],
+        scratch_shapes=scratch,
+        compiler_params=pltpu.CompilerParams(vmem_limit_bytes=LIMIT, **params),
         name=body.__name__,
     )(*args)
-
-
-def rope_base_tables(pos, hd):
-    half = hd // 2
-    inv = jnp.power(1000000.0, -jnp.arange(half, dtype=F32) * (2.0 / hd))
-    angles = pos.astype(F32)[:, None] * inv[None, :]
-    cos, sin = jnp.cos(angles), jnp.sin(angles)
-    return jnp.concatenate([cos, cos], axis=1), jnp.concatenate([-sin, sin], axis=1)
 
 
 def on_plane(hidden_in, seq_lengths, in_gain, w_query, w_key, w_value, q_gain, k_gain, w_out, post_gain,
              w_gate, w_up, w_down, d_out):
     n, nz = lax.axis_size("ctx"), lax.axis_size("fsdp")
-    c, z = lax.axis_index("ctx"), lax.axis_index("fsdp")
     t, dm = hidden_in.shape[1:]
-    half = t // 2
     rows = n * t
     hd = q_gain.shape[0] * n * nz
     ql = w_query.shape[1] // hd // n
@@ -717,91 +815,74 @@
     r_in, r_out, r_down = w_query.shape[0], w_out.shape[0], w_down.shape[0]
     qkv = (ql + 2 * kvl) * hd
     tiles = rows // TILE
-    cfg = dict(n=n, nz=nz, ql=ql, kvl=kvl, hd=hd, ff=ff, eps=1e-6, window=rows // 2 // TILE, slots=6 * n + 6 * nz)
-
-    lengths = seq_lengths[0]
-    ends = jnp.cumsum(lengths)
-    begins = ends - lengths
-    packed = jnp.arange(rows, dtype=jnp.int32)
-    inside = packed[:, None] >= begins[None, :]
-    start = jnp.max(jnp.where(inside, begins[None, :], 0), axis=1)
-    start = jnp.where(packed < ends[-1], start, packed).astype(jnp.int32)
-    pos = packed - start
-    by_block = pos.reshape(2 * n, half)
-    pos_dev = jnp.concatenate([by_block[:n, None], by_block[n:][::-1][:, None]], axis=1).reshape(rows)
-    cos, sin = rope_base_tables(pos_dev, hd)
-    cos, sin = cos.reshape(n, t, hd), sin.reshape(n, t, hd)
-    own = jnp.concatenate([c * half + jnp.arange(half), (2 * n - 1 - c) * half + jnp.arange(half)])
-    valid = (own < ends[-1]).astype(F32)[:, None]
-    db = d_out[0] * valid.astype(BF)
+    cfg = dict(n=n, nz=nz, ql=ql, kvl=kvl, hd=hd, ff=ff, eps=1e-6, window=rows // 2 // TILE, slots=10 * n + 8 * nz)
+
+    inv = 1000000.0 ** (-np.arange(hd // 2) * (2.0 / hd))
+    angles = np.arange(rows)[:, None] * inv[None, :]
+    table = jnp.asarray(np.concatenate([np.cos(angles), np.sin(angles)], axis=1), F32)
+    begins = jnp.cumsum(seq_lengths[0]) - seq_lengths[0]
+    begin_rows = jnp.take(table, begins, axis=0, mode="clip")
+
+    def tiled(gain):
+        return jnp.tile(gain, LANES // gain.shape[0])[None]
+
+    gpack = jnp.concatenate([tiled(in_gain), tiled(post_gain), tiled(q_gain), tiled(k_gain)], axis=0).astype(F32)
     x = hidden_in[0]
-
-    def place(gain, width):
-        wide = jnp.zeros((width,), F32)
-        return lax.dynamic_update_slice(wide, gain.astype(F32), ((c * nz + z) * gain.shape[0],)).reshape(-1, LANES)
-
-    gains = jnp.concatenate([place(in_gain, dm), place(post_gain, dm), place(q_gain, hd), place(k_gain, hd),
-                             jnp.zeros((GAIN_ROWS - 18, LANES), F32)], axis=0)
-
-    def by_device(w):
-        return jnp.transpose(w.reshape(w.shape[0], n, -1), (1, 0, 2))
-
-    wqkv = jnp.concatenate([by_device(w_query), by_device(w_key), by_device(w_value)], axis=2)
-    wgu = jnp.concatenate([by_device(w_gate), by_device(w_up)], axis=2)
-
-    xn, q, k, v, pre, gu_plane, wo, w, gains = call(
-        gather_qkv, cfg,
-        [((n, t, dm), BF), ((tiles, ql, TILE, hd), BF), ((tiles, kvl, TILE, hd), BF), ((tiles, kvl, TILE, hd), BF),
-         ((n, t, (ql + kvl) * hd), F32), ((n, r_in, 2 * ff), BF), ((nz, r_out, dm), BF), ((n, nz, r_in, qkv), BF),
+    smem = pl.BlockSpec(memory_space=pltpu.SMEM)
+    anywhere = pl.BlockSpec(memory_space=pl.ANY)
+
+    def hbm(shape, dtype):
+        return (shape, dtype, anywhere)
+
+    big, low, wide = (n, t, dm), (tiles, TILE, 2 * hd), (tiles, ql, TILE, 2 * hd)
+    pre_w = (ql + kvl) * hd
+    sums = [pltpu.VMEM((n // 2, t, dm), BF)] * 2 + [pltpu.VMEM((n // 2 - 1, t, dm), BF)] * 2 + [pltpu.VMEM((t, dm), F32)]
+    gains_s = [pltpu.VMEM((GAIN_ROWS, LANES), F32), pltpu.VMEM((n, GAIN_ROWS, LANES), F32),
+               pltpu.VMEM((nz, GAIN_ROWS, LANES), F32)]
+    (qx, kx, vx, dax, mo, pre, cs, xn, w, gwo, grad_down, ggu, h_mid, d_hmid, gains, gpost) = call(
+        front, cfg, [smem] + [VMEM] * 12,
+        [hbm(wide, BF), hbm(low, BF), hbm(low, BF), hbm(wide, BF), hbm(big, BF), hbm((n, t, pre_w), F32),
+         hbm((n, t, hd), F32), hbm(big, BF), hbm((n, nz, r_in, qkv), BF), hbm((nz, r_out, dm), BF),
+         hbm((r_down, dm), F32), hbm((n, r_in, 2 * ff), BF), hbm((t, dm), F32), hbm((t, dm), F32),
+         ((GAIN_ROWS, LANES), F32), ((1, dm), F32)],
+        [pltpu.VMEM((n, r_in, qkv), BF), pltpu.VMEM((n, r_in, 2 * ff), BF), pltpu.VMEM((n, nz, r_in, qkv), BF),
+         pltpu.VMEM((nz, r_out, dm), BF), pltpu.VMEM((8, LANES), BF), pltpu.VMEM((n, nz, r_in, 2 * ff), BF),
+         pltpu.VMEM((nz, r_down, dm), BF)] + gains_s
+        + [pltpu.VMEM(big, BF), pltpu.VMEM(big, BF), pltpu.VMEM((t, dm), BF), pltpu.VMEM((n, t, pre_w), F32),
+           pltpu.VMEM((n, t, hd), F32), pltpu.VMEM(wide, BF), pltpu.VMEM(low, BF), pltpu.VMEM(low, BF),
+           pltpu.VMEM((ql * TILE, 2 * hd), F32), pltpu.VMEM((rows, ql * hd), BF),
+           pltpu.VMEM(big, BF), pltpu.VMEM((n, t, ff), BF), pltpu.VMEM((n, t, 2 * ff), BF), pltpu.VMEM((2, t, dm), BF)]
+        + sums
+        + [pltpu.VMEM((t, dm), BF), pltpu.VMEM((t, dm), F32), pltpu.VMEM((t, dm), F32), pltpu.VMEM(wide, BF),
+           pltpu.VMEM((nz, r_out, dm), BF), pltpu.VMEM((nz, r_down, dm), BF), pltpu.VMEM((nz - 1, r_down, dm), BF),
+           pltpu.VMEM((n, nz, r_in, 2 * ff), BF), pltpu.VMEM((nz - 1, n, r_in, 2 * ff), BF),
+           pltpu.VMEM((r_down, dm), F32), pltpu.VMEM((n, r_in, 2 * ff), BF), pltpu.VMEM((1, dm), F32)],
+        1, seq_lengths, x, d_out[0], w_query, w_key, w_value, w_out, w_gate, w_up, w_down, gpack, table, begin_rows)
+
+    block, dx, gwo, ggu, gqkv, small = call(
+        back, cfg, [smem] + [VMEM] * 4 + [anywhere] * 5 + [VMEM] * 2 + [anywhere] * 2 + [VMEM] * 3,
+        [((t, dm), BF), ((t, dm), F32), ((r_out, dm), F32), ((n, r_in, 2 * ff), BF), ((n, r_in, qkv), BF),
          ((GAIN_ROWS, LANES), F32)],
-        [pltpu.VMEM((n, t, dm), BF), pltpu.VMEM((n, GAIN_ROWS, LANES), F32), pltpu.VMEM((nz, GAIN_ROWS, LANES), F32)],
-        1, x, wqkv, wgu, w_out, gains, cos, sin)
-
-    attn, qx, dblk, gu = call(
-        attend, cfg,
-        [((rows, ql * hd), BF), ((tiles, ql, TILE, 2 * hd), BF), ((n, t, dm), BF), ((n, nz, r_in, 2 * ff), BF)],
-        [pltpu.VMEM((tiles, TILE, 2 * hd), BF), pltpu.VMEM((ql * TILE, 2 * hd), F32)],
-        2, q, k, v, start[:, None], db, gu_plane)
-
-    mo, dax, h_mid, d_hmid, gwo, gwd, ggu, gpost = call(
-        feed, cfg,
-        [((n, t, dm), BF), ((tiles, ql, TILE, 2 * hd), BF), ((t, dm), F32), ((t, dm), F32), ((nz, r_out, dm), BF),
-         ((r_down, dm), F32), ((n, r_in, 2 * ff), BF), ((1, dm), F32)],
-        [pltpu.VMEM((nz, r_down, dm), BF), pltpu.VMEM((n, t, dm), BF), pltpu.VMEM((n, t, ff), BF),
-         pltpu.VMEM((n, t, 2 * ff), BF), pltpu.VMEM((n, t, dm), BF),
-         pltpu.VMEM((nz, r_down, dm), BF), pltpu.VMEM((n, nz, r_in, 2 * ff), BF),
-         pltpu.VMEM((nz - 1, r_down, dm), BF), pltpu.VMEM((nz - 1, n, r_in, 2 * ff), BF)]
-        + plane_sum_scratch(n, t, dm) + plane_sum_scratch(n, t, dm) + [pltpu.VMEM((t, dm), BF)],
-        3, attn, x, dblk, wo, gu, w_down, gains)
-
-    dq, dk, dv, block_out, grad_wo, grad_gate, grad_up = call(
-        attend_back, cfg,
-        [((tiles, ql * TILE, hd), F32), ((tiles, TILE, hd), F32), ((tiles, TILE, hd), F32), ((t, dm), BF),
-         ((r_out, dm), F32), ((r_in, n * ff), F32), ((r_in, n * ff), F32)],
-        [pltpu.VMEM((tiles, TILE, 2 * hd), BF), pltpu.VMEM((tiles, TILE, 2 * hd), BF),
-         pltpu.VMEM((TILE, hd), F32), pltpu.VMEM((TILE, hd), F32),
-         pltpu.VMEM((nz - 1, r_out, dm), BF), pltpu.VMEM((n, r_in, 2 * ff), BF)]
-        + plane_sum_scratch(n, t, dm),
-        4, qx, k, v, dax, start[None, :], mo, h_mid, valid, gwo, ggu)
-
-    dx, grad_q, grad_k, grad_v, small = call(
-        head_back, cfg,
-        [((t, dm), F32), ((r_in, n * ql * hd), F32), ((r_in, n * kvl * hd), F32), ((r_in, n * kvl * hd), F32),
-         ((GAIN_ROWS, LANES), F32)],
-        [pltpu.VMEM((n, t, qkv), BF), pltpu.VMEM((n, nz, r_in, qkv), BF), pltpu.VMEM((nz - 1, n, r_in, qkv), BF),
-         pltpu.VMEM((n, r_in, qkv), BF), pltpu.VMEM((n, r_in, qkv), BF),
-         pltpu.VMEM((GAIN_ROWS, LANES), F32), pltpu.VMEM((n, GAIN_ROWS, LANES), F32),
-         pltpu.VMEM((nz, GAIN_ROWS, LANES), F32)]
-        + plane_sum_scratch(n, t, dm),
-        5, pre, dq, dk, dv, cos, sin, gains, xn, w, x, d_hmid, gpost)
-
-    def mine(first, width, share):
-        flat = small[first : first + width // LANES].reshape(width)
-        return lax.dynamic_slice(flat, ((c * nz + z) * share,), (share,))
-
-    return (block_out[None], dx[None], mine(0, dm, in_gain.shape[0]), grad_q, grad_k, grad_v,
-            mine(16, hd, q_gain.shape[0]), mine(17, hd, k_gain.shape[0]), grad_wo,
-            mine(8, dm, post_gain.shape[0]), grad_gate, grad_up, gwd)
+        sums[:4]
+        + [pltpu.VMEM((n, t, pre_w), F32), pltpu.VMEM((n, t, hd), F32), pltpu.VMEM(big, BF),
+           pltpu.VMEM((n, nz, r_in, qkv), BF), pltpu.VMEM((t, dm), F32), pltpu.VMEM((t, dm), F32),
+           pltpu.VMEM((tiles, ql * TILE, hd), F32), pltpu.VMEM((tiles, TILE, hd), F32),
+           pltpu.VMEM((tiles, TILE, hd), F32), pltpu.VMEM((TILE, hd), F32), pltpu.VMEM((TILE, hd), F32),
+           pltpu.VMEM((nz - 1, r_out, dm), BF), pltpu.VMEM((n, r_in, 2 * ff), BF),
+           pltpu.VMEM((n, t, qkv), BF), pltpu.VMEM((n, nz, r_in, qkv), BF), pltpu.VMEM((nz - 1, n, r_in, qkv), BF),
+           pltpu.VMEM((n, r_in, qkv), BF), pltpu.VMEM((n, r_in, qkv), BF)]
+        + gains_s + sums,
+        2, seq_lengths, qx, kx, vx, dax, mo, pre, cs, xn, w, gwo, ggu, h_mid, d_hmid, gains, gpost, x)
+
+    grads = call(
+        finish, cfg, [VMEM] * 7,
+        [((t, dm), BF), ((t, dm), F32), ((1, in_gain.shape[0]), F32), ((r_in, n * ql * hd), F32),
+         ((r_in, n * kvl * hd), F32), ((r_in, n * kvl * hd), F32), ((1, q_gain.shape[0]), F32),
+         ((1, k_gain.shape[0]), F32), ((r_out, dm), F32), ((1, post_gain.shape[0]), F32), ((r_in, n * ff), F32),
+         ((r_in, n * ff), F32), ((r_down, dm), F32)],
+        [], None, block, dx, gwo, grad_down, ggu, gqkv, small)
+    (block, dx, g_in, g_q, g_k, g_v, g_qg, g_kg, g_o, g_post, g_gate, g_up, g_down) = grads
+    return (block[None], dx[None], g_in[0], g_q, g_k, g_v, g_qg[0], g_kg[0], g_o, g_post[0], g_gate, g_up, g_down)
 
 
 epsilon = 1e-06

time: 376 us -> 293 us (0.78)
  Pallas kernels: 331 us -> 281 us
  other arithmetic: 18.1 us -> 2.08 us
  local copies, waits for them, and re-layouts: 19.3 us -> 5.39 us
    pallas_call x5 -> x3, Pallas kernels: 331 us -> 281 us  [call(): pl.pallas_call(functools.partial(body, cfg), out_shape=[jax.ShapeDtypeStr...]
    unnamed x29 -> x0, local copies, waits for them, and re-layouts: 8.93 us -> none
where the time goes in v2:
time: 293 us; the launch traced here: 290 us
  Pallas kernels  281 us (96%)
  local copies, waits for them, and re-layouts  5.39 us (2%)
    pallas_call x3, Pallas kernels, call(): pl.pallas_call(functools.partial(body, cfg), out_shape=[jax.ShapeDtypeStr...  281 us

profile of v2, /device:TPU:0, one launch (start us, length us, event | category | flops | bytes accessed | tf_op | source)
XLA Modules:
  0.0 289.6 jit_solution(12629636112041384049)
XLA Ops:
  0.6 0.8 reduce-window.4
  1.5 0.7 subtract_bitcast_fusion
  2.1 0.7 tile.8
  2.8 0.1 broadcast_in_dim_tile.12
  2.9 0.7 tile.9
  3.5 0.1 broadcast_in_dim_tile.13
  3.6 2.4 gather_fusion
  6.0 0.7 tile.10
  6.6 0.1 broadcast_in_dim_tile.14
  6.8 0.7 tile.11
  7.4 0.1 broadcast_in_dim_tile.15
  7.5 0.6 maximum_convert_fusion.gpack_ref
  8.1 196.5 %front.1 = (bf16[8,2,256,256]{3,2,1,0:T(8,128)(2,1)}, bf16[8,256,256]{2,1,0:T(8,128)(2,1)}, bf16[8,256,256]{2,1,0:T(8,128)(2,1)}, bf16[8,2,256,256]{3,2,1,0:T(8,...) custom-call(s32[1,4]{1,0:T(1,128)} %lengths_ref.3, ...), custom_call_target="tpu_custom_call" | custom-call | tf_op jit(solution)/shard_map/front/pallas_call | solution.py:795
  204.6 80.9 %back.1 = (bf16[256,1024]{1,0:T(8,128)(2,1)}, f32[256,1024]{1,0:T(8,128)}, f32[64,1024]{1,0:T(8,128)}, bf16[8,32,768]{2,1,0:T(8,128)(2,1)}, bf16[8,32,512]{2,1,0:T(8,128)(2,1)}, /*index=5*/f32[24,128]{1,0:T(8,128)}) custom-call(s32[1,4]{1,0:T(1,128)} %lengths_ref.3, bf16[8,2,256,256]{3,2,1,0:T(8,128)(2,1)} %get-tuple-element.48.qx_ref, ...), custom_call_target="tpu_custom_call" | custom-call | tf_op jit(solution)/shard_map/back/pallas_call | solution.py:795
  285.5 3.6 %finish.1 = (bf16[256,1024]{1,0:T(8,128)(2,1)}, f32[256,1024]{1,0:T(8,128)}, f32[1,32]{1,0:T(1,128)}, f32[32,2048]{1,0:T(8,128)}, f32[32,1024]{1,0:T(8,128)}, /*...) custom-call(bf16[256,1024]{1,0:T(8,128)(2,1)} %get-tuple-element.63., ...), custom_call_target="tpu_custom_call" | custom-call | tf_op jit(solution)/shard_map/finish/pallas_call | solution.py:795
  (1 shorter events, 0.0 us)
